TPU v7x, 256 devices: a whole 4x4x8 slice. The times are simulated.
256 devices in a mesh: row: 16 (over y_hi, z), col: 16 (over y_lo, x, core).
Axes of the slice: x: 4, y: 4 (y_hi: 2, y_lo: 2; y = y_hi * 2 + y_lo), z: 8, core: 2. Of those that a mesh axis runs over, the one named last changes fastest.
Arguments:
- tokens: bfloat16 [1024, 8192], P('col', 'row'), may hold values from -6 to 6
- row_order: int32 [1024], P('col'), may hold values from 0 to 1023, as said below
- adapter_id: int32 [1], replicated, may hold values from 0 to 63
- gate_weight: bfloat16 [8192, 28672], P('row', 'col'), may hold values from -0.0625 to 0.0625
- up_weight: bfloat16 [8192, 28672], P('row', 'col'), may hold values from -0.0625 to 0.0625
- down_weight: bfloat16 [28672, 8192], P('col', 'row'), may hold values from -0.03125 to 0.03125
- gate_inner: bfloat16 [64, 8192, 64], P(None, ('row', 'col')), may hold values from -0.0625 to 0.0625
- gate_outer: bfloat16 [64, 64, 28672], P(None, None, ('col', 'row')), may hold values from -0.1796875 to 0.1796875
- up_inner: bfloat16 [64, 8192, 64], P(None, ('row', 'col')), may hold values from -0.0625 to 0.0625
- up_outer: bfloat16 [64, 64, 28672], P(None, None, ('col', 'row')), may hold values from -0.1796875 to 0.1796875
- down_inner: bfloat16 [64, 28672, 64], P(None, ('col', 'row')), may hold values from -0.03125 to 0.03125
- down_outer: bfloat16 [64, 64, 8192], P(None, None, ('row', 'col')), may hold values from -0.1796875 to 0.1796875
Outputs:
- mixed: bfloat16 [1024, 8192], P('col', 'row')
Inputs may be any that keep to these rules, and one draw needn't show every extreme that they name: Within each aligned block of 64 rows, row_order holds every index of that same block exactly once.
All inputs are finite; a program needn't handle non-finite values.
Results may differ from a plain program's by a relative error of at most 0.0071.
Values may be sent and summed in bfloat16 or wider, within the bound.
A program may use at most 128 MiB of HBM per device.

v0:
```python
import jax
import jax.numpy as jnp
from jax import lax
from jax.sharding import PartitionSpec as P


def choose(pool, pick):
    return lax.dynamic_index_in_dim(pool, pick, 0, keepdims=False)


def merge_one(base, inner, outer):
    low = jnp.dot(inner, outer, preferred_element_type=jnp.float32)
    return (base.astype(jnp.float32) + 2.0 * low).astype(jnp.bfloat16)


def body(
    tokens,
    row_order,
    adapter_id,
    gate_weight,
    up_weight,
    down_weight,
    gate_inner,
    gate_outer,
    up_inner,
    up_outer,
    down_inner,
    down_outer,
):
    pick = adapter_id[0]
    inner_gate, inner_up, outer_down = (
        lax.all_gather(choose(gate_inner, pick), "col", axis=0, tiled=True),
        lax.all_gather(choose(up_inner, pick), "col", axis=0, tiled=True),
        lax.all_gather(choose(down_outer, pick), "col", axis=1, tiled=True),
    )
    outer_gate, outer_up, inner_down = (
        lax.all_gather(choose(gate_outer, pick), "row", axis=1, tiled=True),
        lax.all_gather(choose(up_outer, pick), "row", axis=1, tiled=True),
        lax.all_gather(choose(down_inner, pick), "row", axis=0, tiled=True),
    )
    merged_gate = merge_one(gate_weight, inner_gate, outer_gate)
    merged_up = merge_one(up_weight, inner_up, outer_up)
    merged_down = merge_one(down_weight, inner_down, outer_down)
    local_rows = tokens.shape[0]
    ordered = jnp.take(tokens, row_order % local_rows, axis=0)
    gathered = lax.all_gather(ordered, "col", axis=0, tiled=True)
    gate_term = jnp.dot(gathered, merged_gate, preferred_element_type=jnp.float32)
    up_term = jnp.dot(gathered, merged_up, preferred_element_type=jnp.float32)
    gate, up = lax.psum((gate_term, up_term), "row")
    hidden_all = (jax.nn.silu(gate) * up).astype(jnp.bfloat16)
    mixed = lax.psum_scatter(
        jnp.dot(hidden_all, merged_down, preferred_element_type=jnp.float32),
        "col",
        scatter_dimension=0,
        tiled=True,
    )
    return mixed.astype(jnp.bfloat16)


def solution(mesh):
    return jax.shard_map(
        body,
        mesh=mesh,
        in_specs=(
            P("col", "row"),
            P("col"),
            P(),
            P("row", "col"),
            P("row", "col"),
            P("col", "row"),
            P(None, ("row", "col"), None),
            P(None, None, ("col", "row")),
            P(None, ("row", "col"), None),
            P(None, None, ("col", "row")),
            P(None, ("col", "row"), None),
            P(None, None, ("row", "col")),
        ),
        out_specs=P("col", "row"),
        check_vma=False,
    )
```

profile of v0, /device:TPU:1, one launch (start us, length us, event | category | flops | bytes accessed | tf_op | source)
XLA Modules:
  0.0 563.5 jit_solution(7375772770515990551)
XLA Ops:
  6.5 0.0 copy-start
  6.5 0.0 all-gather.8.cloned.1.call-start
  6.5 0.8 compare_and_fusion
  7.3 1.6 gather_fusion
  8.9 0.7 broadcast_select_fusion
  9.6 0.0 all-gather.8.cloned.1.call-update
  9.6 0.0 all-reduce.3.cloned.1.call-start
  10.3 0.0 copy-done
  10.3 0.1 copy.22
  10.5 43.4 %all-gather.1 = bf16[1,64,1792]{1,0,2:T(2,128)(2,1)S(1)} all-gather(bf16[1,64,112]{1,0,2:T(2,128)(2,1)S(1)} %copy.22), channel_id=3, replica_groups=mesh['row'=16,'col'=16] {'row'}, dimensions={2}, use_global_device_ids=true | all-gather | bytes 243712 | tf_op jit(solution)/shard_map/all_gather | solution.py:37
  53.8 0.9 copy.17
  54.7 0.7 constant_dynamic-slice_fusion.2
  55.4 0.1 copy.23
  55.6 35.4 %all-gather.3 = bf16[1,64,1792]{1,0,2:T(2,128)(2,1)S(1)} all-gather(bf16[1,64,112]{1,0,2:T(2,128)(2,1)S(1)} %copy.23), channel_id=5, replica_groups=mesh['row'=16,'col'=16] {'row'}, dimensions={2}, use_global_device_ids=true | all-gather | bytes 243712 | tf_op jit(solution)/shard_map/all_gather | solution.py:38
  91.0 0.9 copy.19
  91.9 0.7 constant_dynamic-slice_fusion.5
  92.6 32.2 %all-gather = bf16[1,512,64]{2,1,0:T(8,128)(2,1)S(1)} all-gather(bf16[1,32,64]{2,1,0:T(8,128)(2,1)S(1)} %constant_dynamic-slice_fusion.5), channel_id=2, replica_groups=mesh['row'=16,'col'=16] {'col'}, dimensions={1}, use_global_device_ids=true | all-gather | bytes 69632 | tf_op jit(solution)/shard_map/all_gather | solution.py:32
  124.8 0.7 constant_dynamic-slice_fusion.3
  125.5 16.6 %all-gather.2 = bf16[1,512,64]{2,1,0:T(8,128)(2,1)S(1)} all-gather(bf16[1,32,64]{2,1,0:T(8,128)(2,1)S(1)} %constant_dynamic-slice_fusion.3), channel_id=4, replica_groups=mesh['row'=16,'col'=16] {'col'}, dimensions={1}, use_global_device_ids=true | all-gather | bytes 69632 | tf_op jit(solution)/shard_map/all_gather | solution.py:33
  142.1 0.0 all-gather.8.cloned.1.call-done
  142.1 0.0 copy-start.1
  142.1 7.3 %fusion.1 = f32[1024,1792]{1,0:T(8,128)} fusion(bf16[1024,512]{1,0:T(8,128)(2,1)} %all-gather.8.cloned.1.call-done, bf16[512,1792]{1,0:T(8,128)(2,1)} %param.15, bf16[1,64,1792]{2,1,0:T(8,128)(2,1)S(1)} %copy.17, bf16[1,512,64]{2,1,0:T(8,128)(2,1)S(1)} %all-gather), kind=kOutput, calls=%fused_computation.6 | convolution fusion | flops 2000158720 | bytes 10518528 | tf_op jit(solution)/shard_map/dot_general | solution.py:47
  149.4 0.0 copy-done.1
  149.4 7.0 %fusion.2 = f32[1024,1792]{1,0:T(8,128)} fusion(bf16[1024,512]{1,0:T(8,128)(2,1)S(1)} %copy-done.1, bf16[512,1792]{1,0:T(8,128)(2,1)} %param.16, bf16[1,64,1792]{2,1,0:T(8,128)(2,1)S(1)} %copy.19, bf16[1,512,64]{2,1,0:T(8,128)(2,1)S(1)} %all-gather.2), kind=kOutput, calls=%fused_computation.7 | convolution fusion | flops 2000158720 | bytes 10518528 | tf_op jit(solution)/shard_map/dot_general | solution.py:48
  156.4 0.0 all-reduce.3.cloned.1.call-update
  156.4 0.0 reduce-scatter.2.cloned.1.call-start
  156.5 0.7 constant_dynamic-slice_fusion.1
  157.2 0.1 copy.24
  157.3 47.7 %all-gather.4 = bf16[1,1792,64]{2,0,1:T(2,128)(2,1)S(1)} all-gather(bf16[1,112,64]{2,0,1:T(2,128)(2,1)S(1)} %copy.24), channel_id=6, replica_groups=mesh['row'=16,'col'=16] {'row'}, dimensions={1}, use_global_device_ids=true | all-gather | bytes 243712 | tf_op jit(solution)/shard_map/all_gather | solution.py:39
  205.0 0.9 copy.21
  205.8 0.7 constant_dynamic-slice_fusion
  206.5 23.4 %all-gather.5 = bf16[1,64,512]{1,2,0:T(8,128)(2,1)S(1)} all-gather(bf16[1,64,32]{1,2,0:T(8,128)(2,1)S(1)} %constant_dynamic-slice_fusion), channel_id=7, replica_groups=mesh['row'=16,'col'=16] {'col'}, dimensions={2}, use_global_device_ids=true | all-gather | bytes 69632 | tf_op jit(solution)/shard_map/all_gather | solution.py:34
  230.0 256.8 %all-reduce.3.cloned.1.call-done = (f32[1024,1792]{1,0:T(8,128)}, f32[1024,1792]{1,0:T(8,128)}) async-done(((f32[1024,1792]{1,0:T(8,128)}, f32[1024,1792]{1,0:T(8,128)}), (f32[1024,1792]{1,0:T(8,128)}, f32[1024,1792]{1,0:T(8,128)})) %all-reduce.3.cloned.1.call-update) | async-done | bytes 14680080 | tf_op jit(solution)/shard_map/psum | solution.py:49
  486.8 9.6 %fusion = f32[1024,512]{1,0:T(8,128)} fusion(f32[1024,1792]{1,0:T(8,128)} %get-tuple-element.5, f32[1024,1792]{1,0:T(8,128)} %get-tuple-element.6, bf16[1792,512]{1,0:T(8,128)(2,1)} %param.17, bf16[1,1792,64]{1,2,0:T(8,128)(2,1)S(1)} %copy.21, bf16[1,64,512]{1,2,0:T(8,128)(2,1)S(1)} %all-gather.5), kind=kOutput, calls=%fused_computation.5 | convolution fusion | flops 2011168768 | bytes 18907136 | tf_op jit(solution)/shard_map/dot_general | solution.py:52
  496.3 0.0 reduce-scatter.2.cloned.1.call-update
  496.4 59.0 %reduce-scatter.2.cloned.1.call-done = f32[64,512]{1,0:T(8,128)} async-done(((f32[1024,512]{1,0:T(8,128)}), f32[64,512]{1,0:T(8,128)}) %reduce-scatter.2.cloned.1.call-update) | async-done | bytes 131088 | tf_op jit(solution)/shard_map/reduce_scatter | solution.py:51
  555.4 1.5 convert_element_type.31
  (2 shorter events, 0.0 us)
Async XLA Ops:
  6.5 3.8 copy-start
  6.5 135.5 %all-gather.8.cloned.1.call-start = ((), (), s32[]{:S(2)}) async-start(), calls=%async_computation.1 | async-start | bytes 1114112 | tf_op jit(solution)/shard_map/all_gather | solution.py:46
  9.6 477.2 %all-reduce.3.cloned.1.call-start = ((), (), s32[]{:S(2)}) async-start(), calls=%async_computation.3 | async-start | bytes 29360128 | tf_op jit(solution)/shard_map/psum | solution.py:49
  142.1 7.4 %copy-start.1 = (bf16[1024,512]{1,0:T(8,128)(2,1)S(1)}, bf16[1024,512]{1,0:T(8,128)(2,1)}, u32[]{:S(2)}) copy-start(bf16[1024,512]{1,0:T(8,128)(2,1)} %all-gather.8.cloned.1.call-done) | copy-start | bytes 3145732
  156.4 399.0 %reduce-scatter.2.cloned.1.call-start = ((), (), s32[]{:S(2)}) async-start(), calls=%async_computation.2 | async-start | bytes 2228224 | tf_op jit(solution)/shard_map/reduce_scatter | solution.py:51
Sparse Core Ops, SparseCore 0:
  9.7 40.2 all-gather.7
  156.5 330.1 all-reduce.2
  496.5 58.8 reduce-scatter.1
where the time goes:
time: 566 us; the launch traced here: 563 us
  waiting for transfers between devices  316 us (56%)
  blocking collectives  199 us (35%)
  matrix products  23.9 us (4%)
  between operations  13.8 us (2%)
  local copies, waits for them, and re-layouts  8.07 us (1%)
    psum x1, waiting for transfers between devices, body(): gate, up = lax.psum((gate_term, up_term), 'row')  257 us
    reduce_scatter x1, waiting for transfers between devices, body(): lax.psum_scatter(jnp.dot(hidden_all, merged_down, preferred_element_type=...  59 us
    all_gather x1, blocking collectives, body(): lax.all_gather(choose(down_inner, pick), 'row', axis=0, tiled=True)  47.7 us
    all_gather x1, blocking collectives, body(): lax.all_gather(choose(gate_outer, pick), 'row', axis=1, tiled=True)  43.4 us
    all_gather x1, blocking collectives, body(): lax.all_gather(choose(up_outer, pick), 'row', axis=1, tiled=True)  35.4 us
    all_gather x1, blocking collectives, body(): lax.all_gather(choose(gate_inner, pick), 'col', axis=0, tiled=True)  32.2 us
    all_gather x1, blocking collectives, body(): lax.all_gather(choose(down_outer, pick), 'col', axis=1, tiled=True)  23.4 us
    all_gather x1, blocking collectives, body(): lax.all_gather(choose(up_inner, pick), 'col', axis=0, tiled=True)  16.6 us
  transfers between devices with their start and end apart: 3, of which 2 were waited for; matrix products, arithmetic and copies ran while one was open for 1% of the time, Pallas kernels for 0%

commit v1 on v0

v1 whole, which is shorter than its diff:
```python
import functools

import jax
import jax.numpy as jnp
from jax import lax
from jax.experimental import pallas as pl
from jax.experimental.pallas import tpu as pltpu
from jax.sharding import PartitionSpec as P

MESH = pl.DeviceIdType.MESH
BF = jnp.bfloat16
F32 = jnp.float32
GROUPS = 7
GW = 256
A_GROUPS = (1, 3, 5, 6)
B_GROUPS = (0, 2, 4)
NA, NB = len(A_GROUPS), len(B_GROUPS)
AGY = (0, 2, 4, 1)
AGZ = (3, 5, 6)
CW, CCW = 0, 1
T00 = (((0,), (0,)), ((), ()))
T11 = (((1,), (1,)), ((), ()))


def dot(a, b, dims=(((1,), (0,)), ((), ()))):
    return lax.dot_general(a, b, dims, preferred_element_type=F32)


def pick_kernel(k_ref, order_ref, tok_ref, gi_ref, ui_ref, di_ref, go_ref, uo_ref, do_ref, rows_ref, inner_ref, outer_ref):
    r = lax.broadcasted_iota(jnp.int32, (64, 128), 0)
    c = lax.broadcasted_iota(jnp.int32, (64, 128), 1)
    left = jnp.where(r == c, 1.0, 0.0).astype(BF)
    right = jnp.where(r + 64 == c, 1.0, 0.0).astype(BF)
    source = lax.broadcasted_iota(jnp.int32, (64, 64), 0)
    one_hot = jnp.where(source == order_ref[...] % 64, 1.0, 0.0).astype(BF)
    rows_ref[...] = dot(one_hot, tok_ref[...], T00).astype(BF).reshape(4, 16, 512)
    inner_ref[0] = (dot(gi_ref[0], left) + dot(ui_ref[0], right)).astype(BF)
    inner_ref[1] = dot(do_ref[0], left, T00).astype(BF)
    outer_ref[0] = (dot(go_ref[0], left, T00) + dot(uo_ref[0], right, T00)).astype(BF)
    outer_ref[1] = dot(di_ref[0], left).astype(BF)


def pick(adapter_id, order, tokens, gi, ui, di, go, uo, do):
    whole = lambda shape: pl.BlockSpec(shape, lambda i, k: (0,) * len(shape))
    chosen = lambda a: pl.BlockSpec((1,) + a.shape[1:], lambda i, k: (k[0], 0, 0))
    return pl.pallas_call(
        pick_kernel,
        out_shape=(
            jax.ShapeDtypeStruct((4, 16, 512), BF),
            jax.ShapeDtypeStruct((2, 32, 128), BF),
            jax.ShapeDtypeStruct((2, 112, 128), BF),
        ),
        grid_spec=pltpu.PrefetchScalarGridSpec(
            num_scalar_prefetch=1,
            grid=(1,),
            in_specs=[whole((1, 64)), whole((64, 512))] + [chosen(a) for a in (gi, ui, di, go, uo, do)],
            out_specs=(whole((4, 16, 512)), whole((2, 32, 128)), whole((2, 112, 128))),
        ),
    )(adapter_id, order.reshape(1, 64), tokens, gi, ui, di, go, uo, do)


def kernel(
    rows_ref, inner_ref, outer_ref, gate_hbm, up_hbm, down_hbm, out_ref,
    wg, wu, wd, x, ibuf, ogu, od, im, part, yrec_a, zrec_a, zrec_b, yrec_b, hid, obuf, orec,
    load_sem, own_sem, x_sem, i_sem, o_sem, gather_send,
    rsz_recv, rsy_recv, agz_recv, agy_recv, ring_send, out_sem,
):
    row, col = lax.axis_index("row"), lax.axis_index("col")
    yh, z = row // 8, row % 8
    chip, core = col // 2, col % 2
    zat = lambda k: (z + k + 8) % 8
    up_dev = (yh * 8 + zat(1), col)
    down_dev = (yh * 8 + zat(-1), col)
    y_dev = ((1 - yh) * 8 + z, col)
    sib_dev = (row, chip * 2 + 1 - core)
    ring_dev = (up_dev, down_dev)

    def remote(src, dst, send, recv, dev):
        return pltpu.make_async_remote_copy(src, dst, send, recv, device_id=dev, device_id_type=MESH)

    def wait_recv(dst, recv):
        remote(dst, dst, gather_send.at[0], recv, y_dev).wait_recv()

    def wait_send(src, send):
        remote(src, src, send, out_sem.at[1], y_dev).wait_send()

    loads = [
        pltpu.make_async_copy(src, dst, load_sem.at[i])
        for i, (src, dst) in enumerate(((gate_hbm, wg), (up_hbm, wu), (down_hbm, wd)))
    ]
    for load in loads:
        load.start()

    barrier = pltpu.get_barrier_semaphore()
    for k in range(1, 16):
        pl.semaphore_signal(barrier, inc=1, device_id=(row, (col + k) % 16), device_id_type=MESH)
    for k in range(1, 8):
        pl.semaphore_signal(barrier, inc=1, device_id=(yh * 8 + zat(k), col), device_id_type=MESH)
    pl.semaphore_signal(barrier, inc=1, device_id=y_dev, device_id_type=MESH)
    pl.semaphore_wait(barrier, 23)

    def o_at(ref, r):
        return ref.at[pl.ds(pl.multiple_of(r * 112, 16), 112)]

    def x_at(chip_, core_):
        return x.at[pl.ds(core_ * 4, 4), pl.ds(pl.multiple_of(chip_ * 16, 16), 16)]

    own = []

    def keep(src, dst, i):
        copy = pltpu.make_async_copy(src, dst, own_sem.at[i])
        copy.start()
        own.append(copy)

    order = (1, 7, 2, 6, 3, 5, 4)
    for n, ref in ((0, ogu), (1, od)):
        src = outer_ref.at[n]
        keep(src, o_at(ref, row), n)
        if n == 0:
            for k in order:
                remote(src, o_at(ref, row), gather_send.at[2 + n], o_sem.at[n, 0, k], (yh * 8 + zat(k), col)).start()
            remote(src, o_at(ref, row), gather_send.at[2 + n], o_sem.at[n, 1, 0], y_dev).start()
            keep(inner_ref, ibuf.at[col], 2)
            for k in order:
                remote(inner_ref, ibuf.at[col], gather_send.at[1], i_sem.at[0, k], (row, (chip + k) % 8 * 2 + core)).start()
            remote(inner_ref, ibuf.at[col], gather_send.at[1], i_sem.at[1, 0], sib_dev).start()
            keep(rows_ref, x_at(chip, core), 3)
            for k in order:
                remote(rows_ref, x_at(chip, core), gather_send.at[0], x_sem.at[0, k], (row, (chip + k) % 8 * 2 + core)).start()
            remote(rows_ref, x_at(chip, core), gather_send.at[0], x_sem.at[1, 0], sib_dev).start()
        else:
            for k in order:
                remote(src, o_at(ref, row), gather_send.at[2 + n], o_sem.at[n, 0, k], (yh * 8 + zat(k), col)).start()
            remote(src, o_at(ref, row), gather_send.at[2 + n], o_sem.at[n, 1, 0], y_dev).start()

    def pass_outer(n, ref):
        for k in order:
            here = o_at(ref, yh * 8 + zat(-k))
            wait_recv(here, o_sem.at[n, 0, k])
            remote(here, here, gather_send.at[2 + n], o_sem.at[n, 1, k], y_dev).start()

    def end_outer(n, ref):
        for k in range(8):
            wait_recv(o_at(ref, (1 - yh) * 8 + zat(-k)), o_sem.at[n, 1, k])

    for k in order:
        here = ibuf.at[(chip + 8 - k) % 8 * 2 + core]
        wait_recv(here, i_sem.at[0, k])
        remote(here, here, gather_send.at[1], i_sem.at[1, k], sib_dev).start()
    pass_outer(0, ogu)
    for k in order:
        here = x_at((chip + 8 - k) % 8, core)
        wait_recv(here, x_sem.at[0, k])
        remote(here, here, gather_send.at[0], x_sem.at[1, k], sib_dev).start()
    for copy in own:
        copy.wait()
    for k in range(8):
        wait_recv(ibuf.at[(chip + 8 - k) % 8 * 2 + 1 - core], i_sem.at[1, k])
    lane = lax.broadcasted_iota(jnp.int32, (512, 128), 1)
    pairs = ibuf[:, 0].reshape(512, 128)
    im[0] = jnp.where(lane < 64, pairs, jnp.zeros_like(pairs))
    im[1] = jnp.where(lane >= 64, pairs, jnp.zeros_like(pairs))
    im[2] = ibuf[:, 1].reshape(512, 128)
    end_outer(0, ogu)
    loads[0].wait()
    loads[1].wait()

    def merge(g):
        factor = ogu[g * GW:(g + 1) * GW]
        for half, w in enumerate((wg, wu)):
            low = dot(im[half], factor, T11)
            cols = slice(g * GW, (g + 1) * GW)
            w[:, cols] = (w[:, cols].astype(F32) + 2.0 * low).astype(BF)

    def merge_down():
        @pl.loop(0, 7)
        def _(i):
            at = pl.ds(pl.multiple_of(i * 256, 256), 256)
            low = dot(od[at], im[2], T11)
            wd[at] = (wd[at].astype(F32) + 2.0 * low).astype(BF)

    def products(g):
        cols = slice(g * GW, (g + 1) * GW)

        @pl.loop(0, 2)
        def _(i):
            rows = x[pl.ds(i * 4, 4)].reshape(512, 512)
            for half, w in enumerate((wg, wu)):
                term = dot(rows, w[:, cols])
                part[g, pl.ds(i * 4, 4), :, :, half * GW:(half + 1) * GW] = term.astype(BF).reshape(4, 2, 64, GW)

    def rs_refs(g):
        if g in A_GROUPS:
            n = A_GROUPS.index(g)
            return zrec_a.at[n], (lambda d: part.at[g, d, yh]), yrec_a.at[n]
        n = B_GROUPS.index(g)
        return zrec_b.at[n], (lambda d: part.at[g, d]), None

    def lanes(half):
        return pl.ds(half * GW, GW)

    def rs_y(g):
        _, _, yrec = rs_refs(g)
        remote(part.at[g, :, 1 - yh], yrec, ring_send.at[1, g], rsy_recv.at[g], y_dev).start()

    def rs_1(g):
        zrec, at, yrec = rs_refs(g)
        d = zat(4)
        if yrec is not None:
            wait_recv(yrec, rsy_recv.at[g])
            at(d)[...] = (at(d)[...].astype(F32) + yrec[d].astype(F32)).astype(BF)
        for way in (CW, CCW):
            remote(
                at(d).at[..., lanes(way)], zrec.at[way, 0].at[..., lanes(way)],
                ring_send.at[0, g], rsz_recv.at[g, way, 0], ring_dev[way],
            ).start()

    def rs_s(g, s):
        zrec, at, yrec = rs_refs(g)
        for way in (CW, CCW):
            d = zat(5 - s if way == CW else s - 5)
            got = zrec.at[way, s - 2]
            spot = at(d)
            if s == 2:
                wait_recv(got.at[..., lanes(way)], rsz_recv.at[g, way, 0])
                for half in (0, 1):
                    total = spot[..., lanes(half)].astype(F32)
                    if yrec is not None:
                        total = total + yrec[d, :, lanes(half)].astype(F32)
                    if half == way:
                        total = total + got[..., lanes(half)].astype(F32)
                    if half == way or yrec is not None:
                        spot[..., lanes(half)] = total.astype(BF)
            else:
                wait_recv(got, rsz_recv.at[g, way, s - 2])
                total = spot[...].astype(F32) + got[...].astype(F32)
                if yrec is not None:
                    total = total + yrec[d].astype(F32)
                spot[...] = total.astype(BF)
            remote(spot, zrec.at[way, s - 1], ring_send.at[0, g], rsz_recv.at[g, way, s - 1], ring_dev[way]).start()

    def rs_end(g):
        zrec, at, _ = rs_refs(g)
        for way in (CW, CCW):
            wait_recv(zrec.at[way, 3], rsz_recv.at[g, way, 3])

    def rs_pass(g):
        rs_end(g)
        zrec, at, _ = rs_refs(g)
        away = part.at[g, z, 1 - yh]
        total = away[...].astype(F32) + zrec[CW, 3, 1 - yh].astype(F32) + zrec[CCW, 3, 1 - yh].astype(F32)
        away[...] = total.astype(BF)
        remote(away, yrec_b.at[B_GROUPS.index(g)], ring_send.at[1, g], rsy_recv.at[g], y_dev).start()

    def hidden(g):
        if g in A_GROUPS:
            rs_end(g)
            zrec, at, yrec = rs_refs(g)
            terms = (part.at[g, z, yh], yrec.at[z], zrec.at[CW, 3], zrec.at[CCW, 3])
        else:
            n = B_GROUPS.index(g)
            wait_recv(yrec_b.at[n], rsy_recv.at[g])
            terms = (part.at[g, z, yh], zrec_b.at[n, CW, 3, yh], zrec_b.at[n, CCW, 3, yh], yrec_b.at[n])
        sums = []
        for half in (0, 1):
            total = terms[0][:, lanes(half)].astype(F32)
            for term in terms[1:]:
                total = total + term[:, lanes(half)].astype(F32)
            sums.append(total)
        gate, up = sums
        hid[z, yh, :, g * GW:(g + 1) * GW] = (gate / (1.0 + jnp.exp(-gate)) * up).astype(BF)

    def h_at(g, d, s=1, way=None):
        lo, n = (g * GW, GW) if s < 4 else (g * GW + way * GW // 2, GW // 2)
        if g in AGY:
            return hid.at[d, yh, :, pl.ds(lo, n)]
        return hid.at[d, :, :, pl.ds(lo, n)]

    def ag_y(g, d):
        ref = hid.at[d, yh, :, pl.ds(g * GW, GW)]
        remote(ref, ref, ring_send.at[3, g], agy_recv.at[g], y_dev).start()

    def ag_1(g):
        if g in AGY:
            ag_y(g, z)
        else:
            wait_recv(hid.at[z, 1 - yh, :, pl.ds(g * GW, GW)], agy_recv.at[g])
        for way in (CW, CCW):
            ref = h_at(g, z)
            remote(ref, ref, ring_send.at[2, g], agz_recv.at[g, way, 0], ring_dev[way]).start()

    def ag_s(g, s):
        for way in (CW, CCW):
            d = zat(1 - s if way == CW else s - 1)
            wait_recv(h_at(g, d), agz_recv.at[g, way, s - 2])
            ref = h_at(g, d, s, way)
            remote(ref, ref, ring_send.at[2, g], agz_recv.at[g, way, s - 1], ring_dev[way]).start()
            if g in AGY:
                ag_y(g, d)

    def ag_end(g):
        for way in (CW, CCW):
            wait_recv(h_at(g, zat(4), 4, way), agz_recv.at[g, way, 3])
        if g in AGY:
            ag_y(g, zat(4))

    def ag_fin(g):
        wait_recv(hid.at[:, 1 - yh, :, pl.ds(g * GW, GW)], agy_recv.at[g])

    def down(d):
        term = dot(hid[d].reshape(128, GROUPS * GW), wd[...])
        obuf[d] = term.astype(BF).reshape(8, 16, 512)

        @pl.loop(0, 8)
        def _(j):
            to = j * 2 + d // 4

            @pl.when(to != col)
            def _():
                remote(
                    obuf.at[d, j], orec.at[(to + 15 - col) % 16, d % 4],
                    out_sem.at[0], out_sem.at[1], (row, to),
                ).start()

    def start(g):
        merge(g)
        products(g)
        if g in A_GROUPS:
            rs_y(g)
        else:
            rs_1(g)

    for k in range(8):
        wait_recv(x_at((chip + 8 - k) % 8, 1 - core), x_sem.at[1, k])

    b0, b1, b2 = B_GROUPS
    a0, a1, a2, a3 = A_GROUPS
    start(b0)
    start(a0)
    start(b1)
    start(b2)
    rs_s(b0, 2)
    start(a1)
    rs_s(b1, 2)
    start(a2)
    rs_s(b2, 2)
    start(a3)
    pass_outer(1, od)
    for g in B_GROUPS:
        rs_s(g, 3)
    rs_1(a0)
    end_outer(1, od)
    loads[2].wait()
    merge_down()
    for g in B_GROUPS:
        rs_s(g, 4)
    rs_s(a0, 2)
    rs_1(a1)
    for g in B_GROUPS:
        rs_pass(g)
    rs_s(a0, 3)
    rs_s(a1, 2)
    rs_s(a0, 4)
    rs_s(a1, 3)
    for g in B_GROUPS:
        hidden(g)
        ag_1(g)
    rs_s(a1, 4)
    rs_1(a2)
    for g in B_GROUPS:
        ag_s(g, 2)
    hidden(a0)
    ag_1(a0)
    rs_s(a2, 2)
    hidden(a1)
    remote_own(hid, a1, z, yh, agy_recv, ring_send, remote, y_dev)
    for g in B_GROUPS:
        ag_s(g, 3)
    ag_s(a0, 2)
    rs_1(a3)
    rs_s(a2, 3)
    for g in B_GROUPS:
        ag_s(g, 4)
    rs_s(a3, 2)
    ag_s(a0, 3)
    ag_1(a1)
    rs_s(a2, 4)
    rs_s(a3, 3)
    for g in B_GROUPS:
        ag_end(g)
    ag_s(a0, 4)
    ag_s(a1, 2)
    rs_s(a3, 4)
    hidden(a2)
    remote_own(hid, a2, z, yh, agy_recv, ring_send, remote, y_dev)
    ag_end(a0)
    ag_s(a1, 3)
    hidden(a3)
    remote_own(hid, a3, z, yh, agy_recv, ring_send, remote, y_dev)
    ag_1(a2)
    ag_s(a1, 4)
    ag_1(a3)
    for g in AGY:
        ag_fin(g)
    ag_s(a2, 2)
    ag_s(a3, 2)
    ag_end(a1)
    down(z)
    down(zat(1))
    down(zat(-1))
    ag_s(a2, 3)
    ag_s(a3, 3)
    down(zat(2))
    down(zat(-2))
    ag_s(a2, 4)
    ag_s(a3, 4)
    down(zat(3))
    down(zat(-3))
    ag_end(a2)
    ag_end(a3)
    down(zat(4))

    wait_recv(orec, out_sem.at[1])
    for p in range(4):
        total = obuf[core * 4 + p, chip].astype(F32)
        for k in range(15):
            total = total + orec[k, p].astype(F32)
        out_ref[p] = total.astype(BF)

    wait_send(orec, out_sem.at[0])
    wait_send(orec, gather_send.at[0])
    wait_send(ibuf.at[pl.ds(0, 15)], gather_send.at[1])
    wait_send(ogu.at[pl.ds(0, 15 * 112)], gather_send.at[2])
    wait_send(od.at[pl.ds(0, 15 * 112)], gather_send.at[3])
    for g in range(GROUPS):
        cols = pl.ds(g * GW, GW)
        if g in A_GROUPS:
            wait_send(part.at[g, pl.ds(0, 7), 0], ring_send.at[0, g])
            wait_send(part.at[g, :, 0], ring_send.at[1, g])
        else:
            wait_send(part.at[g, pl.ds(0, 7)], ring_send.at[0, g])
            wait_send(part.at[g, 0, 0], ring_send.at[1, g])
        if g in AGY:
            wait_send(hid.at[pl.ds(0, 7), 0, :, cols], ring_send.at[2, g])
            wait_send(hid.at[:, 0, :, cols], ring_send.at[3, g])
        else:
            wait_send(hid.at[pl.ds(0, 7), :, :, cols], ring_send.at[2, g])
            wait_send(hid.at[0, 0, :, cols], ring_send.at[3, g])


def remote_own(hid, g, z, yh, agy_recv, ring_send, remote, y_dev):
    ref = hid.at[z, yh, :, pl.ds(g * GW, GW)]
    remote(ref, ref, ring_send.at[3, g], agy_recv.at[g], y_dev).start()


def layer(rows, inner, outer, gate_weight, up_weight, down_weight):
    vmem = pl.BlockSpec(memory_space=pltpu.VMEM)
    hbm = pl.BlockSpec(memory_space=pl.ANY)
    dma = pltpu.SemaphoreType.DMA
    return pl.pallas_call(
        kernel,
        out_shape=jax.ShapeDtypeStruct((4, 16, 512), BF),
        in_specs=[vmem, vmem, vmem, hbm, hbm, hbm],
        out_specs=vmem,
        scratch_shapes=[
            pltpu.VMEM((512, 1792), BF),
            pltpu.VMEM((512, 1792), BF),
            pltpu.VMEM((1792, 512), BF),
            pltpu.VMEM((8, 128, 512), BF),
            pltpu.VMEM((16, 2, 32, 128), BF),
            pltpu.VMEM((1792, 128), BF),
            pltpu.VMEM((1792, 128), BF),
            pltpu.VMEM((3, 512, 128), BF),
            pltpu.VMEM((GROUPS, 8, 2, 64, 2 * GW), BF),
            pltpu.VMEM((NA, 8, 64, 2 * GW), BF),
            pltpu.VMEM((NA, 2, 4, 64, 2 * GW), BF),
            pltpu.VMEM((NB, 2, 4, 2, 64, 2 * GW), BF),
            pltpu.VMEM((NB, 64, 2 * GW), BF),
            pltpu.VMEM((8, 2, 64, GROUPS * GW), BF),
            pltpu.VMEM((8, 8, 16, 512), BF),
            pltpu.VMEM((15, 4, 16, 512), BF),
            dma((3,)),
            dma((4,)),
            dma((2, 8)),
            dma((2, 8)),
            dma((2, 2, 8)),
            dma((4,)),
            dma((GROUPS, 2, 4)),
            dma((GROUPS,)),
            dma((GROUPS, 2, 4)),
            dma((GROUPS,)),
            dma((4, GROUPS)),
            dma((2,)),
        ],
        compiler_params=pltpu.CompilerParams(
            collective_id=0, has_side_effects=True, vmem_limit_bytes=56 * 2**20
        ),
    )(rows, inner, outer, gate_weight, up_weight, down_weight)


def body(
    tokens, row_order, adapter_id, gate_weight, up_weight, down_weight,
    gate_inner, gate_outer, up_inner, up_outer, down_inner, down_outer,
):
    rows, inner, outer = pick(
        adapter_id, row_order, tokens, gate_inner, up_inner, down_inner, gate_outer, up_outer, down_outer
    )
    return layer(rows, inner, outer, gate_weight, up_weight, down_weight).reshape(64, 512)


def solution(mesh):
    return jax.shard_map(
        body,
        mesh=mesh,
        in_specs=(
            P("col", "row"),
            P("col"),
            P(),
            P("row", "col"),
            P("row", "col"),
            P("col", "row"),
            P(None, ("row", "col"), None),
            P(None, None, ("col", "row")),
            P(None, ("row", "col"), None),
            P(None, None, ("col", "row")),
            P(None, ("col", "row"), None),
            P(None, None, ("row", "col")),
        ),
        out_specs=P("col", "row"),
        check_vma=False,
    )
```

time: 566 us -> 163 us (0.29)
  waiting for transfers between devices: 316 us -> 0 us
  blocking collectives: 199 us -> 0 us
  Pallas kernels: 0 us -> 156 us
  matrix products: 23.9 us -> 0 us
  between operations: 13.8 us -> 0.75 us
    psum x1 -> x0, waiting for transfers between devices: 257 us -> none  [body(): gate, up = lax.psum((gate_term, up_term), 'row')]
    all_gather x6 -> x0, blocking collectives: 199 us -> none  [the longest x1 47.7 us: body(): lax.all_gather(choose(down_inner, pick), 'row', axis=0, tiled=True)]
    pallas_call x0 -> x2, Pallas kernels: none -> 156 us  [the longest x1 154 us: layer(): pl.pallas_call(kernel, out_shape=jax.ShapeDtypeStruct((4, 16, 512), BF),...]
    reduce_scatter x1 -> x0, waiting for transfers between devices: 59 us -> none  [body(): lax.psum_scatter(jnp.dot(hidden_all, merged_down, preferred_element_type=...]
    dot_general x3 -> x0, matrix products: 23.9 us -> none  [the longest x1 9.57 us: body(): jnp.dot(hidden_all, merged_down, preferred_element_type=jnp.float32)]
  transfers between devices with their start and end apart: 3 -> 0, of which waited for: 2 -> 0; matrix products, arithmetic and copies ran while one was open for 1% -> 0% of each run, Pallas kernels for 0% -> 0%
where the time goes in v1:
time: 163 us; the launch traced here: 162 us
  Pallas kernels  156 us (96%)
  local copies, waits for them, and re-layouts  5.57 us (3%)
    pallas_call x1, Pallas kernels, layer(): pl.pallas_call(kernel, out_shape=jax.ShapeDtypeStruct((4, 16, 512), BF),...  154 us
    unnamed x5, local copies, waits for them, and re-layouts  5.57 us

profile of v1, /device:TPU:1, one launch (start us, length us, event | category | flops | bytes accessed | tf_op | source)
XLA Modules:
  0.0 162.3 jit_solution(13134728817574825604)
XLA Ops:
  0.0 0.0 copy-start
  0.7 2.4 %copy.14.do_ref = bf16[64,64,32]{2,1,0:T(8,128)(2,1)} copy(bf16[64,64,32]{1,2,0:T(8,128)(2,1)} %param.23) | data formatting | bytes 524288 | tf_op args[11]
  3.1 0.0 copy-done
  3.1 1.7 %copy.13.di_ref = bf16[64,112,64]{2,1,0:T(8,128)(2,1)} copy(bf16[64,112,64]{1,2,0:T(8,128)(2,1)S(1)} %copy-done) | data formatting | bytes 1835008 | tf_op args[10]
  4.8 1.7 %shard_map.118 = (bf16[4,16,512]{2,1,0:T(8,128)(2,1)}, bf16[2,32,128]{2,1,0:T(8,128)(2,1)}, bf16[2,112,128]{2,1,0:T(8,128)(2,1)}) custom-call(s32[1]{0:T(128)S(6)} %copy.16.k_ref, s32[1,64]{1,0:T(1,128)} %bitcast.3, bf16[64,512]{1,0:T(8,128)(2,1)} %tok_ref.1, bf16[64,32,64]{2,1,0:T(8,128)(2,1)} %gi_ref.1, bf16[64,32,64]{2,1,0:T(8,128)(2,1)} %ui_ref.1, ...), custom_call_target="tpu_custom_call" | custom-call | tf_op jit(solution)/shard_map/pallas_call | solution.py:46
  6.6 154.2 %shard_map.119 = bf16[4,16,512]{2,1,0:T(8,128)(2,1)} custom-call(bf16[4,16,512]{2,1,0:T(8,128)(2,1)} %get-tuple-element.8.rows_ref, bf16[2,32,128]{2,1,0:T(8,128)(2,1)} %get-tuple-element.9.inner_ref, bf16[2,112,128]{2,1,0:T(8,128)(2,1)} %get-tuple-element.10.outer_ref, bf16[512,1792]{1,0:T(8,128)(2,1)} %gate_hbm.1, bf16[512,1792]{1,0:T(8,128)(2,1)} %up_hbm.1, ...), custom_call_target="tpu_custom_call" | custom-call | tf_op jit(solution)/shard_map/pallas_call | solution.py:460
  160.8 1.5 copy.17
Async XLA Ops:
  0.0 3.1 %copy-start = (bf16[64,112,64]{1,2,0:T(8,128)(2,1)S(1)}, bf16[64,112,64]{1,2,0:T(8,128)(2,1)}, u32[]{:S(2)}) copy-start(bf16[64,112,64]{1,2,0:T(8,128)(2,1)} %param.22) | copy-start | bytes 2752516

commit v2 on v1

v2 whole, which is shorter than its diff:
```python
import functools

import jax
import jax.numpy as jnp
from jax import lax
from jax.experimental import pallas as pl
from jax.experimental.pallas import tpu as pltpu
from jax.sharding import PartitionSpec as P

MESH = pl.DeviceIdType.MESH
BF = jnp.bfloat16
F32 = jnp.float32
GROUPS = 7
GW = 256
A_GROUPS = (1, 3, 5)
B_GROUPS = (0, 2, 4, 6)
NA, NB = len(A_GROUPS), len(B_GROUPS)
AGY = (0, 2, 4, 6)
AGZ = (1, 3, 5)
CW, CCW = 0, 1
ORDER = (
    ("start", 0), ("start", 4), ("start", 2), ("start", 6), ("rs", 0, 2), ("start", 3), ("od",), ("rs", 4, 2),
    ("rs", 2, 2), ("rs", 6, 2), ("start", 1), ("mdown",), ("rs", 0, 3), ("rs", 4, 3), ("rs", 3, 1), ("start", 5),
    ("rs", 2, 3), ("rs", 6, 3), ("rs", 0, 4), ("rs", 1, 1), ("rs", 4, 4), ("rs", 3, 2), ("rs", 2, 4), ("rs", 6, 4),
    ("rs", 5, 1), ("pass", 0), ("rs", 1, 2), ("pass", 4), ("rs", 3, 3), ("pass", 2), ("pass", 6), ("hid", 0),
    ("rs", 5, 2), ("hid", 4), ("rs", 1, 3), ("hid", 2), ("rs", 3, 4), ("ag", 0, 2), ("hid", 6), ("rs", 5, 3),
    ("ag", 4, 2), ("rs", 1, 4), ("ag", 2, 2), ("hid", 3), ("ag", 0, 3), ("ag", 6, 2), ("rs", 5, 4), ("ag", 3, 1),
    ("ag", 4, 3), ("hid", 1), ("ag", 2, 3), ("ag", 0, 4), ("ag", 6, 3), ("hid", 5), ("ag", 1, 1), ("ag", 3, 2),
    ("ag", 4, 4), ("ag", 2, 4), ("ag", 0, 5), ("ag", 6, 4), ("ag", 5, 1), ("ag", 1, 2), ("ag", 3, 3), ("ag", 4, 5),
    ("ag", 2, 5), ("ag", 6, 5), ("fin", 0), ("ag", 5, 2), ("ag", 1, 3), ("fin", 4), ("fin", 2), ("ag", 3, 4),
    ("fin", 6), ("down", 0), ("ag", 5, 3), ("down", 1), ("ag", 3, 5), ("ag", 1, 4), ("down", 2), ("ag", 5, 4),
    ("down", 3), ("ag", 1, 5), ("ag", 5, 5), ("down", 4),
)
T00 = (((0,), (0,)), ((), ()))
T11 = (((1,), (1,)), ((), ()))


def dot(a, b, dims=(((1,), (0,)), ((), ()))):
    return lax.dot_general(a, b, dims, preferred_element_type=F32)


def kernel(
    pick_ref, order_ref, tokens_ref, gi_hbm, ui_hbm, di_hbm, go_hbm, uo_hbm, do_hbm, gate_hbm, up_hbm, down_hbm, out_ref,
    gi, ui, di, go, uo, do,
    wg, wu, wd, x, ibuf, ogu, od, im, part, yrec_a, zrec_a, zrec_b, yrec_b, hid, obuf, orec,
    load_sem, x_sem, i_sem, o_sem, gather_send,
    rsz_recv, rsy_recv, agz_recv, agy_recv, ring_send, out_sem,
):
    row, col = lax.axis_index("row"), lax.axis_index("col")
    yh, z = row // 8, row % 8
    chip, core = col // 2, col % 2
    zat = lambda k: (z + k + 8) % 8
    up_dev = (yh * 8 + zat(1), col)
    down_dev = (yh * 8 + zat(-1), col)
    y_dev = ((1 - yh) * 8 + z, col)
    sib_dev = (row, chip * 2 + 1 - core)
    ring_dev = (up_dev, down_dev)

    def remote(src, dst, send, recv, dev):
        return pltpu.make_async_remote_copy(src, dst, send, recv, device_id=dev, device_id_type=MESH)

    def wait_recv(dst, recv):
        remote(dst, dst, gather_send.at[0], recv, y_dev).wait_recv()

    def wait_send(src, send):
        remote(src, src, send, out_sem.at[1], y_dev).wait_send()

    pools = ((go_hbm, go), (uo_hbm, uo), (gi_hbm, gi), (ui_hbm, ui), (di_hbm, di), (do_hbm, do))
    weights = ((gate_hbm, wg), (up_hbm, wu), (down_hbm, wd))
    loads = [pltpu.make_async_copy(src, dst, load_sem.at[i]) for i, (src, dst) in enumerate(pools + weights)]
    for load in loads:
        load.start()

    barrier = pltpu.get_barrier_semaphore()
    for k in range(1, 16):
        pl.semaphore_signal(barrier, inc=1, device_id=(row, (col + k) % 16), device_id_type=MESH)
    for k in range(1, 8):
        pl.semaphore_signal(barrier, inc=1, device_id=(yh * 8 + zat(k), col), device_id_type=MESH)
    pl.semaphore_signal(barrier, inc=1, device_id=y_dev, device_id_type=MESH)

    def o_at(ref, r):
        return ref.at[pl.ds(pl.multiple_of(r * 112, 16), 112)]

    def x_at(chip_, core_):
        return x.at[pl.ds(core_ * 4, 4), pl.ds(pl.multiple_of(chip_ * 16, 16), 16)]

    k = pick_ref[0]
    r128 = lax.broadcasted_iota(jnp.int32, (64, 128), 0)
    c128 = lax.broadcasted_iota(jnp.int32, (64, 128), 1)
    left = jnp.where(r128 == c128, 1.0, 0.0).astype(BF)
    right = jnp.where(r128 + 64 == c128, 1.0, 0.0).astype(BF)
    one_hot = jnp.where(lax.broadcasted_iota(jnp.int32, (64, 64), 0) == order_ref[...] % 64, 1.0, 0.0).astype(BF)
    x_at(chip, core)[...] = dot(one_hot, tokens_ref[...], T00).astype(BF).reshape(4, 16, 512)
    loads[0].wait()
    loads[1].wait()
    o_at(ogu, row)[...] = (dot(go[k], left, T00) + dot(uo[k], right, T00)).astype(BF)
    loads[2].wait()
    loads[3].wait()
    ibuf[col, 0] = (dot(gi[k], left) + dot(ui[k], right)).astype(BF)
    loads[4].wait()
    loads[5].wait()
    ibuf[col, 1] = dot(do[k], left).astype(BF)
    o_at(od, row)[...] = dot(di[k], left, T00).astype(BF)
    pl.semaphore_wait(barrier, 23)

    far = (4, 3, 5, 2, 6, 1, 7)
    near = (1, 7, 2, 6, 3, 5, 4)

    def z_send(n, ref):
        here = o_at(ref, row)
        for k in far:
            remote(here, here, gather_send.at[2 + n], o_sem.at[n, 0, k], (yh * 8 + zat(k), col)).start()
        remote(here, here, gather_send.at[2 + n], o_sem.at[n, 1, 0], y_dev).start()

    def col_send(here, n, sem):
        for k in near:
            remote(here, here, gather_send.at[n], sem.at[0, k], (row, (chip + k) % 8 * 2 + core)).start()
        remote(here, here, gather_send.at[n], sem.at[1, 0], sib_dev).start()

    def z_pass(n, ref):
        for k in near:
            here = o_at(ref, yh * 8 + zat(-k))
            wait_recv(here, o_sem.at[n, 0, k])
            remote(here, here, gather_send.at[2 + n], o_sem.at[n, 1, k], y_dev).start()

    def z_end(n, ref):
        for k in range(8):
            wait_recv(o_at(ref, (1 - yh) * 8 + zat(-k)), o_sem.at[n, 1, k])

    def col_pass(at, n, sem):
        for k in near:
            here = at((chip + 8 - k) % 8, core)
            wait_recv(here, sem.at[0, k])
            remote(here, here, gather_send.at[n], sem.at[1, k], sib_dev).start()

    def col_end(at, n, sem):
        for k in range(8):
            wait_recv(at((chip + 8 - k) % 8, 1 - core), sem.at[1, k])

    i_at = lambda chip_, core_: ibuf.at[chip_ * 2 + core_]
    z_send(0, ogu)
    col_send(i_at(chip, core), 1, i_sem)
    col_send(x_at(chip, core), 0, x_sem)
    z_send(1, od)
    col_pass(i_at, 1, i_sem)
    z_pass(0, ogu)
    col_pass(x_at, 0, x_sem)
    col_end(i_at, 1, i_sem)
    lane = lax.broadcasted_iota(jnp.int32, (512, 128), 1)
    pairs = ibuf[:, 0].reshape(512, 128)
    im[0] = jnp.where(lane < 64, pairs, jnp.zeros_like(pairs))
    im[1] = jnp.where(lane >= 64, pairs, jnp.zeros_like(pairs))
    im[2] = ibuf[:, 1].reshape(512, 128)
    loads[6].wait()
    loads[7].wait()
    z_end(0, ogu)
    col_end(x_at, 0, x_sem)

    def merge(g):
        factor = ogu[g * GW:(g + 1) * GW]
        for half, w in enumerate((wg, wu)):
            low = dot(im[half], factor, T11)
            cols = slice(g * GW, (g + 1) * GW)
            w[:, cols] = (w[:, cols].astype(F32) + 2.0 * low).astype(BF)

    def merge_down():
        z_end(1, od)
        loads[8].wait()

        @pl.loop(0, 7)
        def _(i):
            at = pl.ds(pl.multiple_of(i * 256, 256), 256)
            low = dot(od[at], im[2], T11)
            wd[at] = (wd[at].astype(F32) + 2.0 * low).astype(BF)

    def products(g):
        cols = slice(g * GW, (g + 1) * GW)

        @pl.loop(0, 2)
        def _(i):
            rows = x[pl.ds(i * 4, 4)].reshape(512, 512)
            for half, w in enumerate((wg, wu)):
                term = dot(rows, w[:, cols])
                part[g, pl.ds(i * 4, 4), :, :, half * GW:(half + 1) * GW] = term.astype(BF).reshape(4, 2, 64, GW)

    def rs_refs(g):
        if g in A_GROUPS:
            n = A_GROUPS.index(g)
            return zrec_a.at[n], (lambda d: part.at[g, d, yh]), yrec_a.at[n]
        n = B_GROUPS.index(g)
        return zrec_b.at[n], (lambda d: part.at[g, d]), None

    def lanes(half):
        return pl.ds(half * GW, GW)

    def rs_y(g):
        _, _, yrec = rs_refs(g)
        for k in (4, 3, 5, 2, 6, 1, 7, 0):
            d = zat(k)
            remote(part.at[g, d, 1 - yh], yrec.at[d], ring_send.at[1, g], rsy_recv.at[g, k], y_dev).start()

    def y_wait(g, k):
        _, _, yrec = rs_refs(g)
        wait_recv(yrec.at[zat(k)], rsy_recv.at[g, k])

    def rs_1(g):
        zrec, at, yrec = rs_refs(g)
        d = zat(4)
        if yrec is not None:
            y_wait(g, 4)
            at(d)[...] = (at(d)[...].astype(F32) + yrec[d].astype(F32)).astype(BF)
        for way in (CW, CCW):
            remote(
                at(d).at[..., lanes(way)], zrec.at[way, 0].at[..., lanes(way)],
                ring_send.at[0, g], rsz_recv.at[g, way, 0], ring_dev[way],
            ).start()

    def rs_s(g, s):
        zrec, at, yrec = rs_refs(g)
        for way in (CW, CCW):
            d = zat(5 - s if way == CW else s - 5)
            if yrec is not None:
                y_wait(g, 5 - s if way == CW else s + 3)
            got = zrec.at[way, s - 2]
            spot = at(d)
            if s == 2:
                wait_recv(got.at[..., lanes(way)], rsz_recv.at[g, way, 0])
                for half in (0, 1):
                    total = spot[..., lanes(half)].astype(F32)
                    if yrec is not None:
                        total = total + yrec[d, :, lanes(half)].astype(F32)
                    if half == way:
                        total = total + got[..., lanes(half)].astype(F32)
                    if half == way or yrec is not None:
                        spot[..., lanes(half)] = total.astype(BF)
            else:
                wait_recv(got, rsz_recv.at[g, way, s - 2])
                total = spot[...].astype(F32) + got[...].astype(F32)
                if yrec is not None:
                    total = total + yrec[d].astype(F32)
                spot[...] = total.astype(BF)
            remote(spot, zrec.at[way, s - 1], ring_send.at[0, g], rsz_recv.at[g, way, s - 1], ring_dev[way]).start()

    def rs_end(g):
        zrec, at, _ = rs_refs(g)
        for way in (CW, CCW):
            wait_recv(zrec.at[way, 3], rsz_recv.at[g, way, 3])

    def rs_pass(g):
        rs_end(g)
        zrec, at, _ = rs_refs(g)
        away = part.at[g, z, 1 - yh]
        total = away[...].astype(F32) + zrec[CW, 3, 1 - yh].astype(F32) + zrec[CCW, 3, 1 - yh].astype(F32)
        away[...] = total.astype(BF)
        remote(away, yrec_b.at[B_GROUPS.index(g)], ring_send.at[1, g], rsy_recv.at[g, 0], y_dev).start()

    def hidden(g):
        if g in A_GROUPS:
            rs_end(g)
            y_wait(g, 0)
            zrec, at, yrec = rs_refs(g)
            terms = (part.at[g, z, yh], yrec.at[z], zrec.at[CW, 3], zrec.at[CCW, 3])
        else:
            n = B_GROUPS.index(g)
            wait_recv(yrec_b.at[n], rsy_recv.at[g, 0])
            terms = (part.at[g, z, yh], zrec_b.at[n, CW, 3, yh], zrec_b.at[n, CCW, 3, yh], yrec_b.at[n])
        sums = []
        for half in (0, 1):
            total = terms[0][:, lanes(half)].astype(F32)
            for term in terms[1:]:
                total = total + term[:, lanes(half)].astype(F32)
            sums.append(total)
        gate, up = sums
        hid[z, yh, :, g * GW:(g + 1) * GW] = (gate / (1.0 + jnp.exp(-gate)) * up).astype(BF)
        ag_y(g, z)
        if g in AGY:
            ag_z(g)

    def h_at(g, d, s=1, way=None):
        lo, n = (g * GW, GW) if s < 4 else (g * GW + way * GW // 2, GW // 2)
        if g in AGY:
            return hid.at[d, yh, :, pl.ds(lo, n)]
        return hid.at[d, :, :, pl.ds(lo, n)]

    def ag_y(g, d):
        ref = hid.at[d, yh, :, pl.ds(g * GW, GW)]
        remote(ref, ref, ring_send.at[3, g], agy_recv.at[g], y_dev).start()

    def ag_z(g):
        for way in (CW, CCW):
            ref = h_at(g, z)
            remote(ref, ref, ring_send.at[2, g], agz_recv.at[g, way, 0], ring_dev[way]).start()

    def ag_1(g):
        wait_recv(hid.at[z, 1 - yh, :, pl.ds(g * GW, GW)], agy_recv.at[g])
        ag_z(g)

    def ag_s(g, s):
        for way in (CW, CCW):
            d = zat(1 - s if way == CW else s - 1)
            wait_recv(h_at(g, d), agz_recv.at[g, way, s - 2])
            ref = h_at(g, d, s, way)
            remote(ref, ref, ring_send.at[2, g], agz_recv.at[g, way, s - 1], ring_dev[way]).start()
            if g in AGY:
                ag_y(g, d)

    def ag_end(g):
        for way in (CW, CCW):
            wait_recv(h_at(g, zat(4), 4, way), agz_recv.at[g, way, 3])
        if g in AGY:
            ag_y(g, zat(4))

    def ag_fin(g):
        wait_recv(hid.at[:, 1 - yh, :, pl.ds(g * GW, GW)], agy_recv.at[g])

    def down(d):
        term = dot(hid[d].reshape(128, GROUPS * GW), wd[...])
        obuf[d] = term.astype(BF).reshape(8, 16, 512)

        @pl.loop(0, 8)
        def _(j):
            to = j * 2 + d // 4

            @pl.when(to != col)
            def _():
                remote(
                    obuf.at[d, j], orec.at[(to + 15 - col) % 16, d % 4],
                    out_sem.at[0], out_sem.at[1], (row, to),
                ).start()

    def start(g):
        merge(g)
        products(g)
        if g in A_GROUPS:
            rs_y(g)
        else:
            rs_1(g)

    def rs(g, s):
        rs_1(g) if s == 1 else rs_s(g, s)

    def ag(g, s):
        ag_1(g) if s == 1 else ag_end(g) if s == 5 else ag_s(g, s)

    def rows_done(k):
        for d in (k,) if k in (0, 4) else (k, -k):
            down(zat(d))

    tasks = {
        "start": start, "rs": rs, "pass": rs_pass, "hid": hidden, "ag": ag, "fin": ag_fin,
        "od": lambda: z_pass(1, od), "mdown": merge_down, "down": rows_done,
    }
    for name, *rest in ORDER:
        tasks[name](*rest)

    wait_recv(orec, out_sem.at[1])
    for p in range(4):
        total = obuf[core * 4 + p, chip].astype(F32)
        for k in range(15):
            total = total + orec[k, p].astype(F32)
        out_ref[p] = total.astype(BF)

    wait_send(orec, out_sem.at[0])
    wait_send(orec, gather_send.at[0])
    wait_send(ibuf.at[pl.ds(0, 15)], gather_send.at[1])
    wait_send(ogu.at[pl.ds(0, 15 * 112)], gather_send.at[2])
    wait_send(od.at[pl.ds(0, 15 * 112)], gather_send.at[3])
    for g in range(GROUPS):
        cols = pl.ds(g * GW, GW)
        if g in A_GROUPS:
            wait_send(part.at[g, pl.ds(0, 7), 0], ring_send.at[0, g])
            wait_send(part.at[g, :, 0], ring_send.at[1, g])
        else:
            wait_send(part.at[g, pl.ds(0, 7)], ring_send.at[0, g])
            wait_send(part.at[g, 0, 0], ring_send.at[1, g])
        if g in AGY:
            wait_send(hid.at[pl.ds(0, 7), 0, :, cols], ring_send.at[2, g])
            wait_send(hid.at[:, 0, :, cols], ring_send.at[3, g])
        else:
            wait_send(hid.at[pl.ds(0, 7), :, :, cols], ring_send.at[2, g])
            wait_send(hid.at[0, 0, :, cols], ring_send.at[3, g])


def layer(pick, order, tokens, *arrays):
    vmem = pl.BlockSpec(memory_space=pltpu.VMEM)
    hbm = pl.BlockSpec(memory_space=pl.ANY)
    smem = pl.BlockSpec(memory_space=pltpu.SMEM)
    dma = pltpu.SemaphoreType.DMA
    return pl.pallas_call(
        kernel,
        out_shape=jax.ShapeDtypeStruct((4, 16, 512), BF),
        in_specs=[smem, vmem, vmem] + [hbm] * 9,
        out_specs=vmem,
        scratch_shapes=[pltpu.VMEM(a.shape, BF) for a in arrays[:6]] + [
            pltpu.VMEM((512, 1792), BF),
            pltpu.VMEM((512, 1792), BF),
            pltpu.VMEM((1792, 512), BF),
            pltpu.VMEM((8, 128, 512), BF),
            pltpu.VMEM((16, 2, 32, 128), BF),
            pltpu.VMEM((1792, 128), BF),
            pltpu.VMEM((1792, 128), BF),
            pltpu.VMEM((3, 512, 128), BF),
            pltpu.VMEM((GROUPS, 8, 2, 64, 2 * GW), BF),
            pltpu.VMEM((NA, 8, 64, 2 * GW), BF),
            pltpu.VMEM((NA, 2, 4, 64, 2 * GW), BF),
            pltpu.VMEM((NB, 2, 4, 2, 64, 2 * GW), BF),
            pltpu.VMEM((NB, 64, 2 * GW), BF),
            pltpu.VMEM((8, 2, 64, GROUPS * GW), BF),
            pltpu.VMEM((8, 8, 16, 512), BF),
            pltpu.VMEM((15, 4, 16, 512), BF),
            dma((9,)),
            dma((2, 8)),
            dma((2, 8)),
            dma((2, 2, 8)),
            dma((4,)),
            dma((GROUPS, 2, 4)),
            dma((GROUPS, 8)),
            dma((GROUPS, 2, 4)),
            dma((GROUPS,)),
            dma((4, GROUPS)),
            dma((2,)),
        ],
        compiler_params=pltpu.CompilerParams(
            collective_id=0, has_side_effects=True, vmem_limit_bytes=56 * 2**20
        ),
    )(pick, order, tokens, *arrays)


def body(
    tokens, row_order, adapter_id, gate_weight, up_weight, down_weight,
    gate_inner, gate_outer, up_inner, up_outer, down_inner, down_outer,
):
    swap = lambda a: jnp.swapaxes(a, 1, 2)
    return layer(
        adapter_id, row_order.reshape(1, 64), tokens,
        gate_inner, up_inner, swap(down_inner), gate_outer, up_outer, swap(down_outer),
        gate_weight, up_weight, down_weight,
    ).reshape(64, 512)


def solution(mesh):
    return jax.shard_map(
        body,
        mesh=mesh,
        in_specs=(
            P("col", "row"),
            P("col"),
            P(),
            P("row", "col"),
            P("row", "col"),
            P("col", "row"),
            P(None, ("row", "col"), None),
            P(None, None, ("col", "row")),
            P(None, ("row", "col"), None),
            P(None, None, ("col", "row")),
            P(None, ("col", "row"), None),
            P(None, None, ("row", "col")),
        ),
        out_specs=P("col", "row"),
        check_vma=False,
    )
```

time: 163 us -> 131 us (0.80)
  Pallas kernels: 156 us -> 129 us
  local copies, waits for them, and re-layouts: 5.57 us -> 1.47 us
    pallas_call x1, Pallas kernels: 154 us -> 129 us  [layer(): pl.pallas_call(kernel, out_shape=jax.ShapeDtypeStruct((4, 16, 512), BF),...]
    unnamed x5 -> x1, local copies, waits for them, and re-layouts: 5.57 us -> 1.47 us
    pallas_call x1 -> x0, Pallas kernels: 1.74 us -> none  [pick(): pl.pallas_call(pick_kernel, out_shape=(jax.ShapeDtypeStruct((4, 16, 512),...]
where the time goes in v2:
time: 131 us
  Pallas kernels  129 us (98%)
  local copies, waits for them, and re-layouts  1.47 us (1%)
    pallas_call x1, Pallas kernels, layer(): pl.pallas_call(kernel, out_shape=jax.ShapeDtypeStruct((4, 16, 512), BF),...  129 us

profile of v2, /device:TPU:1, one launch (start us, length us, event | category | flops | bytes accessed | tf_op | source)
XLA Modules:
  0.0 131.1 jit_solution(10395217761236367318)
XLA Ops:
  0.7 128.9 %shard_map.118 = bf16[4,16,512]{2,1,0:T(8,128)(2,1)} custom-call(s32[1]{0:T(128)S(6)} %copy.14.pick_ref, s32[1,64]{1,0:T(1,128)} %bitcast.7, bf16[64,512]{1,0:T(8,128)(2,1)} %tokens_ref.1, bf16[64,32,64]{2,1,0:T(8,128)(2,1)} %gi_hbm.1, bf16[64,32,64]{2,1,0:T(8,128)(2,1)} %ui_hbm.1, bf16[64,64,112]{2,1,0:T(8,128)(2,1)} %bitcast.4, ...), custom_call_target="tpu_custom_call" | custom-call | tf_op jit(solution)/shard_map/pallas_call | solution.py:389
  129.6 1.5 %copy.15 = bf16[64,512]{1,0:T(8,128)(2,1)} copy(bf16[64,512]{1,0:T(8,128)(2,1)} %bitcast.6) | data formatting | bytes 131072

commit v3 on v2

--- a/solution.py
+++ b/solution.py
@@ -19,17 +19,17 @@
 AGZ = (1, 3, 5)
 CW, CCW = 0, 1
 ORDER = (
-    ("start", 0), ("start", 4), ("start", 2), ("start", 6), ("rs", 0, 2), ("start", 3), ("od",), ("rs", 4, 2),
-    ("rs", 2, 2), ("rs", 6, 2), ("start", 1), ("mdown",), ("rs", 0, 3), ("rs", 4, 3), ("rs", 3, 1), ("start", 5),
-    ("rs", 2, 3), ("rs", 6, 3), ("rs", 0, 4), ("rs", 1, 1), ("rs", 4, 4), ("rs", 3, 2), ("rs", 2, 4), ("rs", 6, 4),
-    ("rs", 5, 1), ("pass", 0), ("rs", 1, 2), ("pass", 4), ("rs", 3, 3), ("pass", 2), ("pass", 6), ("hid", 0),
-    ("rs", 5, 2), ("hid", 4), ("rs", 1, 3), ("hid", 2), ("rs", 3, 4), ("ag", 0, 2), ("hid", 6), ("rs", 5, 3),
-    ("ag", 4, 2), ("rs", 1, 4), ("ag", 2, 2), ("hid", 3), ("ag", 0, 3), ("ag", 6, 2), ("rs", 5, 4), ("ag", 3, 1),
-    ("ag", 4, 3), ("hid", 1), ("ag", 2, 3), ("ag", 0, 4), ("ag", 6, 3), ("hid", 5), ("ag", 1, 1), ("ag", 3, 2),
-    ("ag", 4, 4), ("ag", 2, 4), ("ag", 0, 5), ("ag", 6, 4), ("ag", 5, 1), ("ag", 1, 2), ("ag", 3, 3), ("ag", 4, 5),
-    ("ag", 2, 5), ("ag", 6, 5), ("fin", 0), ("ag", 5, 2), ("ag", 1, 3), ("fin", 4), ("fin", 2), ("ag", 3, 4),
-    ("fin", 6), ("down", 0), ("ag", 5, 3), ("down", 1), ("ag", 3, 5), ("ag", 1, 4), ("down", 2), ("ag", 5, 4),
-    ("down", 3), ("ag", 1, 5), ("ag", 5, 5), ("down", 4),
+    ("start", 2), ("ipass",), ("tout",), ("start", 4), ("start", 5), ("start", 6), ("start", 0), ("rs", 2, 2),
+    ("start", 3), ("rs", 5, 1), ("rs", 4, 2), ("rs", 6, 2), ("rs", 5, 2), ("rs", 2, 3), ("start", 1), ("rs", 0, 2),
+    ("rs", 3, 1), ("rs", 6, 3), ("rs", 4, 3), ("rs", 5, 3), ("rs", 0, 3), ("rs", 1, 1), ("rs", 2, 4), ("rs", 4, 4),
+    ("tmid",), ("gpass",), ("rs", 0, 4), ("od",), ("rs", 1, 2), ("pass", 2), ("rs", 5, 4), ("rs", 3, 2), ("pass", 4),
+    ("gend",), ("rs", 6, 4), ("pass", 0), ("rs", 1, 3), ("mdown",), ("tend",), ("hid", 2), ("hid", 4), ("rs", 3, 3),
+    ("hid", 0), ("pass", 6), ("hid", 5), ("rs", 1, 4), ("ag", 2, 2), ("ag", 4, 2), ("rs", 3, 4), ("ag", 0, 2),
+    ("hid", 6), ("hid", 1), ("ag", 5, 1), ("ag", 2, 3), ("hid", 3), ("ag", 0, 3), ("ag", 6, 2), ("ag", 1, 1),
+    ("ag", 5, 2), ("ag", 3, 1), ("ag", 6, 3), ("ag", 2, 4), ("ag", 4, 3), ("ag", 1, 2), ("down", 0), ("ag", 0, 4),
+    ("ag", 3, 2), ("ag", 2, 5), ("ag", 6, 4), ("ag", 5, 3), ("ag", 4, 4), ("ag", 1, 3), ("ag", 3, 3), ("down", 1),
+    ("ag", 5, 4), ("ag", 6, 5), ("down", 2), ("ag", 1, 4), ("ag", 0, 5), ("ag", 3, 4), ("ag", 4, 5), ("ag", 5, 5),
+    ("down", 3), ("ag", 1, 5), ("ag", 3, 5), ("down", 4),
 )
 T00 = (((0,), (0,)), ((), ()))
 T11 = (((1,), (1,)), ((), ()))
@@ -42,9 +42,9 @@
 def kernel(
     pick_ref, order_ref, tokens_ref, gi_hbm, ui_hbm, di_hbm, go_hbm, uo_hbm, do_hbm, gate_hbm, up_hbm, down_hbm, out_ref,
     gi, ui, di, go, uo, do,
-    wg, wu, wd, x, ibuf, ogu, od, im, part, yrec_a, zrec_a, zrec_b, yrec_b, hid, obuf, orec,
-    load_sem, x_sem, i_sem, o_sem, gather_send,
-    rsz_recv, rsy_recv, agz_recv, agy_recv, ring_send, out_sem,
+    wg, wu, wd, x, ibuf, ogu, od, im, tsend, trec, tall, tbig, part, yrec_a, zrec_a, zrec_b, yrec_b, hid, obuf, orec,
+    load_sem, x_sem, i_sem, o_sem, t_sem, gather_send,
+    rsz_recv, rsy_recv, agz_recv, agy_recv, ring_send, out_sem, out_recv,
 ):
     row, col = lax.axis_index("row"), lax.axis_index("col")
     yh, z = row // 8, row % 8
@@ -74,12 +74,14 @@
     barrier = pltpu.get_barrier_semaphore()
     for k in range(1, 16):
         pl.semaphore_signal(barrier, inc=1, device_id=(row, (col + k) % 16), device_id_type=MESH)
-    for k in range(1, 8):
-        pl.semaphore_signal(barrier, inc=1, device_id=(yh * 8 + zat(k), col), device_id_type=MESH)
-    pl.semaphore_signal(barrier, inc=1, device_id=y_dev, device_id_type=MESH)
-
-    def o_at(ref, r):
-        return ref.at[pl.ds(pl.multiple_of(r * 112, 16), 112)]
+    for k in range(1, 16):
+        pl.semaphore_signal(barrier, inc=1, device_id=((row + k) % 16, col), device_id_type=MESH)
+
+    def g_at(r):
+        return ogu.at[pl.ds(pl.multiple_of(r * 112, 16), 112)]
+
+    def d_at(r):
+        return od.at[r]
 
     def x_at(chip_, core_):
         return x.at[pl.ds(core_ * 4, 4), pl.ds(pl.multiple_of(chip_ * 16, 16), 16)]
@@ -93,21 +95,22 @@
     x_at(chip, core)[...] = dot(one_hot, tokens_ref[...], T00).astype(BF).reshape(4, 16, 512)
     loads[0].wait()
     loads[1].wait()
-    o_at(ogu, row)[...] = (dot(go[k], left, T00) + dot(uo[k], right, T00)).astype(BF)
+    g_at(row)[...] = (dot(go[k], left, T00) + dot(uo[k], right, T00)).astype(BF)
     loads[2].wait()
     loads[3].wait()
     ibuf[col, 0] = (dot(gi[k], left) + dot(ui[k], right)).astype(BF)
     loads[4].wait()
     loads[5].wait()
-    ibuf[col, 1] = dot(do[k], left).astype(BF)
-    o_at(od, row)[...] = dot(di[k], left, T00).astype(BF)
-    pl.semaphore_wait(barrier, 23)
+    ibuf[col, 1] = (dot(do[k], left) + dot(do[k], right)).astype(BF)
+    low, high = dot(di[k], left, T00), dot(di[k], right, T00)[64:112]
+    od[row] = (low[0:64] + jnp.concatenate([high, jnp.zeros((16, 128), F32)], axis=0)).astype(BF)
+    pl.semaphore_wait(barrier, 30)
 
     far = (4, 3, 5, 2, 6, 1, 7)
     near = (1, 7, 2, 6, 3, 5, 4)
 
-    def z_send(n, ref):
-        here = o_at(ref, row)
+    def z_send(n, at):
+        here = at(row)
         for k in far:
             remote(here, here, gather_send.at[2 + n], o_sem.at[n, 0, k], (yh * 8 + zat(k), col)).start()
         remote(here, here, gather_send.at[2 + n], o_sem.at[n, 1, 0], y_dev).start()
@@ -117,15 +120,15 @@
             remote(here, here, gather_send.at[n], sem.at[0, k], (row, (chip + k) % 8 * 2 + core)).start()
         remote(here, here, gather_send.at[n], sem.at[1, 0], sib_dev).start()
 
-    def z_pass(n, ref):
+    def z_pass(n, at):
         for k in near:
-            here = o_at(ref, yh * 8 + zat(-k))
+            here = at(yh * 8 + zat(-k))
             wait_recv(here, o_sem.at[n, 0, k])
             remote(here, here, gather_send.at[2 + n], o_sem.at[n, 1, k], y_dev).start()
 
-    def z_end(n, ref):
+    def z_end(n, at):
         for k in range(8):
-            wait_recv(o_at(ref, (1 - yh) * 8 + zat(-k)), o_sem.at[n, 1, k])
+            wait_recv(at((1 - yh) * 8 + zat(-k)), o_sem.at[n, 1, k])
 
     def col_pass(at, n, sem):
         for k in near:
@@ -138,40 +141,61 @@
             wait_recv(at((chip + 8 - k) % 8, 1 - core), sem.at[1, k])
 
     i_at = lambda chip_, core_: ibuf.at[chip_ * 2 + core_]
-    z_send(0, ogu)
+    col_send(x_at(chip, core), 0, x_sem)
+    z_send(0, g_at)
     col_send(i_at(chip, core), 1, i_sem)
-    col_send(x_at(chip, core), 0, x_sem)
-    z_send(1, od)
-    col_pass(i_at, 1, i_sem)
-    z_pass(0, ogu)
+    z_send(1, d_at)
     col_pass(x_at, 0, x_sem)
-    col_end(i_at, 1, i_sem)
-    lane = lax.broadcasted_iota(jnp.int32, (512, 128), 1)
-    pairs = ibuf[:, 0].reshape(512, 128)
-    im[0] = jnp.where(lane < 64, pairs, jnp.zeros_like(pairs))
-    im[1] = jnp.where(lane >= 64, pairs, jnp.zeros_like(pairs))
-    im[2] = ibuf[:, 1].reshape(512, 128)
     loads[6].wait()
     loads[7].wait()
-    z_end(0, ogu)
     col_end(x_at, 0, x_sem)
 
-    def merge(g):
-        factor = ogu[g * GW:(g + 1) * GW]
-        for half, w in enumerate((wg, wu)):
-            low = dot(im[half], factor, T11)
-            cols = slice(g * GW, (g + 1) * GW)
-            w[:, cols] = (w[:, cols].astype(F32) + 2.0 * low).astype(BF)
+    t_role = (yh == col // 8) & (z // 4 == core)
+    t_from = lambda j: yh * 8 + j * 2 + z // 4
+
+    def t_out():
+        col_end(i_at, 1, i_sem)
+        lane = lax.broadcasted_iota(jnp.int32, (512, 128), 1)
+        im[0] = ibuf[:, 0].reshape(512, 128)
+        narrow = ibuf[:, 1].reshape(512, 128)
+        im[1] = jnp.where(lane < 64, narrow, jnp.zeros_like(narrow))
+        im[2] = jnp.where(lane >= 64, narrow, jnp.zeros_like(narrow))
+        tsend[...] = dot(x_at(chip, core)[...].reshape(64, 512), im[0]).reshape(4, 16, 128)
+        for p in range(4):
+            to = col // 8 * 8 + core * 4 + p
+
+            @pl.when(to != row)
+            def _():
+                remote(tsend.at[p], trec.at[(to + 15 - row) % 16], t_sem.at[0], t_sem.at[1], (to, col)).start()
+
+    def t_mid():
+        @pl.when(t_role)
+        def _():
+            wait_recv(trec, t_sem.at[1])
+            total = tsend[z % 4]
+            for k in range(15):
+                total = total + trec[k]
+            mine = tall.at[chip % 4]
+            mine[...] = total.astype(BF)
+            for k in range(1, 16):
+                remote(mine, mine, t_sem.at[2], t_sem.at[3 + chip % 4], (row, (col + k) % 16)).start()
+
+    def t_end():
+        for j in range(4):
+            @pl.when(t_from(j) != col)
+            def _():
+                wait_recv(tall.at[j], t_sem.at[3 + j])
 
     def merge_down():
-        z_end(1, od)
+        z_end(1, d_at)
         loads[8].wait()
 
-        @pl.loop(0, 7)
-        def _(i):
-            at = pl.ds(pl.multiple_of(i * 256, 256), 256)
-            low = dot(od[at], im[2], T11)
-            wd[at] = (wd[at].astype(F32) + 2.0 * low).astype(BF)
+        @pl.loop(0, 16)
+        def _(r):
+            for first, size, n in ((0, 64, 1), (64, 48, 2)):
+                at = pl.ds(pl.multiple_of(r * 112 + first, 16), size)
+                low = dot(od[r, 0:size], im[n], T11)
+                wd[at] = (wd[at].astype(F32) + 2.0 * low).astype(BF)
 
     def products(g):
         cols = slice(g * GW, (g + 1) * GW)
@@ -265,14 +289,17 @@
             wait_recv(yrec_b.at[n], rsy_recv.at[g, 0])
             terms = (part.at[g, z, yh], zrec_b.at[n, CW, 3, yh], zrec_b.at[n, CCW, 3, yh], yrec_b.at[n])
         sums = []
+        pair = tall[...].reshape(64, 128)
+        lane = lax.broadcasted_iota(jnp.int32, (64, 128), 1)
         for half in (0, 1):
             total = terms[0][:, lanes(half)].astype(F32)
             for term in terms[1:]:
                 total = total + term[:, lanes(half)].astype(F32)
-            sums.append(total)
+            one = jnp.where((lane < 64) if half == 0 else (lane >= 64), pair, jnp.zeros_like(pair))
+            sums.append(total + 2.0 * dot(one, ogu[g * GW:(g + 1) * GW], T11))
         gate, up = sums
         hid[z, yh, :, g * GW:(g + 1) * GW] = (gate / (1.0 + jnp.exp(-gate)) * up).astype(BF)
-        ag_y(g, z)
+        ag_y(g, 0)
         if g in AGY:
             ag_z(g)
 
@@ -282,17 +309,20 @@
             return hid.at[d, yh, :, pl.ds(lo, n)]
         return hid.at[d, :, :, pl.ds(lo, n)]
 
-    def ag_y(g, d):
-        ref = hid.at[d, yh, :, pl.ds(g * GW, GW)]
-        remote(ref, ref, ring_send.at[3, g], agy_recv.at[g], y_dev).start()
+    def ag_y(g, k):
+        ref = hid.at[zat(k), yh, :, pl.ds(g * GW, GW)]
+        remote(ref, ref, ring_send.at[3, g], agy_recv.at[g, k % 8], y_dev).start()
 
     def ag_z(g):
         for way in (CW, CCW):
             ref = h_at(g, z)
             remote(ref, ref, ring_send.at[2, g], agz_recv.at[g, way, 0], ring_dev[way]).start()
 
+    def ag_y_wait(g, k):
+        wait_recv(hid.at[zat(k), 1 - yh, :, pl.ds(g * GW, GW)], agy_recv.at[g, k % 8])
+
     def ag_1(g):
-        wait_recv(hid.at[z, 1 - yh, :, pl.ds(g * GW, GW)], agy_recv.at[g])
+        ag_y_wait(g, 0)
         ag_z(g)
 
     def ag_s(g, s):
@@ -302,34 +332,37 @@
             ref = h_at(g, d, s, way)
             remote(ref, ref, ring_send.at[2, g], agz_recv.at[g, way, s - 1], ring_dev[way]).start()
             if g in AGY:
-                ag_y(g, d)
+                ag_y(g, 1 - s if way == CW else s - 1)
 
     def ag_end(g):
         for way in (CW, CCW):
             wait_recv(h_at(g, zat(4), 4, way), agz_recv.at[g, way, 3])
         if g in AGY:
-            ag_y(g, zat(4))
-
-    def ag_fin(g):
-        wait_recv(hid.at[:, 1 - yh, :, pl.ds(g * GW, GW)], agy_recv.at[g])
-
-    def down(d):
-        term = dot(hid[d].reshape(128, GROUPS * GW), wd[...])
-        obuf[d] = term.astype(BF).reshape(8, 16, 512)
-
-        @pl.loop(0, 8)
-        def _(j):
-            to = j * 2 + d // 4
-
-            @pl.when(to != col)
-            def _():
-                remote(
-                    obuf.at[d, j], orec.at[(to + 15 - col) % 16, d % 4],
-                    out_sem.at[0], out_sem.at[1], (row, to),
-                ).start()
+            ag_y(g, 4)
+
+    def down(*offsets):
+        places = [zat(k) for k in offsets]
+        n = len(places)
+        for g in AGY:
+            for k in offsets:
+                ag_y_wait(g, k)
+        rows = [hid[d].reshape(128, GROUPS * GW) for d in places]
+        term = dot(rows[0] if n == 1 else jnp.concatenate(rows, axis=0), wd[...])
+        for m, d in enumerate(places):
+            obuf[d] = term[m * 128:(m + 1) * 128].astype(BF).reshape(8, 16, 512)
+        for d in places:
+            @pl.loop(0, 8)
+            def _(j):
+                to = j * 2 + d // 4
+
+                @pl.when(to != col)
+                def _():
+                    remote(
+                        obuf.at[d, j], orec.at[(to + 15 - col) % 16, d % 4],
+                        out_sem.at[0], out_recv.at[d % 4], (row, to),
+                    ).start()
 
     def start(g):
-        merge(g)
         products(g)
         if g in A_GROUPS:
             rs_y(g)
@@ -343,28 +376,48 @@
         ag_1(g) if s == 1 else ag_end(g) if s == 5 else ag_s(g, s)
 
     def rows_done(k):
-        for d in (k,) if k in (0, 4) else (k, -k):
-            down(zat(d))
+        down(*((k,) if k in (0, 4) else (k, -k)))
 
     tasks = {
-        "start": start, "rs": rs, "pass": rs_pass, "hid": hidden, "ag": ag, "fin": ag_fin,
-        "od": lambda: z_pass(1, od), "mdown": merge_down, "down": rows_done,
+        "start": start, "rs": rs, "pass": rs_pass, "hid": hidden, "ag": ag,
+        "ipass": lambda: col_pass(i_at, 1, i_sem), "gpass": lambda: z_pass(0, g_at), "gend": lambda: z_end(0, g_at),
+        "tout": t_out, "tmid": t_mid, "tend": t_end,
+        "od": lambda: z_pass(1, d_at), "mdown": merge_down, "down": rows_done,
     }
     for name, *rest in ORDER:
         tasks[name](*rest)
 
-    wait_recv(orec, out_sem.at[1])
-    for p in range(4):
-        total = obuf[core * 4 + p, chip].astype(F32)
-        for k in range(15):
-            total = total + orec[k, p].astype(F32)
-        out_ref[p] = total.astype(BF)
+    for k in (0, 1, 7, 2, 6, 3, 5, 4):
+        d = zat(k)
+        p = d % 4
+
+        @pl.when(d // 4 == core)
+        def _():
+            wait_recv(orec.at[:, p], out_recv.at[p])
+            total = obuf[d, chip].astype(F32)
+            for n in range(15):
+                total = total + orec[n, p].astype(F32)
+            out_ref[p] = total.astype(BF)
 
     wait_send(orec, out_sem.at[0])
     wait_send(orec, gather_send.at[0])
     wait_send(ibuf.at[pl.ds(0, 15)], gather_send.at[1])
     wait_send(ogu.at[pl.ds(0, 15 * 112)], gather_send.at[2])
-    wait_send(od.at[pl.ds(0, 15 * 112)], gather_send.at[3])
+    wait_send(od.at[pl.ds(0, 15)], gather_send.at[3])
+    sent = col // 8 * 8 + core * 4
+
+    @pl.when((row >= sent) & (row < sent + 4))
+    def _():
+        wait_send(tsend.at[pl.ds(0, 3)], t_sem.at[0])
+
+    @pl.when((row < sent) | (row >= sent + 4))
+    def _():
+        wait_send(tsend, t_sem.at[0])
+
+    @pl.when(t_role)
+    def _():
+        wait_send(tbig, t_sem.at[2])
+
     for g in range(GROUPS):
         cols = pl.ds(g * GW, GW)
         if g in A_GROUPS:
@@ -398,8 +451,12 @@
             pltpu.VMEM((8, 128, 512), BF),
             pltpu.VMEM((16, 2, 32, 128), BF),
             pltpu.VMEM((1792, 128), BF),
-            pltpu.VMEM((1792, 128), BF),
+            pltpu.VMEM((16, 64, 128), BF),
             pltpu.VMEM((3, 512, 128), BF),
+            pltpu.VMEM((4, 16, 128), F32),
+            pltpu.VMEM((15, 16, 128), F32),
+            pltpu.VMEM((4, 16, 128), BF),
+            pltpu.VMEM((15, 16, 128), BF),
             pltpu.VMEM((GROUPS, 8, 2, 64, 2 * GW), BF),
             pltpu.VMEM((NA, 8, 64, 2 * GW), BF),
             pltpu.VMEM((NA, 2, 4, 64, 2 * GW), BF),
@@ -412,13 +469,15 @@
             dma((2, 8)),
             dma((2, 8)),
             dma((2, 2, 8)),
+            dma((7,)),
             dma((4,)),
             dma((GROUPS, 2, 4)),
             dma((GROUPS, 8)),
             dma((GROUPS, 2, 4)),
-            dma((GROUPS,)),
+            dma((GROUPS, 8)),
             dma((4, GROUPS)),
             dma((2,)),
+            dma((4,)),
         ],
         compiler_params=pltpu.CompilerParams(
             collective_id=0, has_side_effects=True, vmem_limit_bytes=56 * 2**20

time: 131 us -> 122 us (0.931)
  Pallas kernels: 129 us -> 119 us
    pallas_call x1, Pallas kernels: 129 us -> 119 us  [layer(): pl.pallas_call(kernel, out_shape=jax.ShapeDtypeStruct((4, 16, 512), BF),...]
where the time goes in v3:
time: 122 us; the launch traced here: 121 us
  Pallas kernels  119 us (98%)
  local copies, waits for them, and re-layouts  1.47 us (1%)
    pallas_call x1, Pallas kernels, layer(): pl.pallas_call(kernel, out_shape=jax.ShapeDtypeStruct((4, 16, 512), BF),...  119 us

profile of v3, /device:TPU:1, one launch (start us, length us, event | category | flops | bytes accessed | tf_op | source)
XLA Modules:
  0.0 121.4 jit_solution(14639807320111029437)
XLA Ops:
  0.7 119.3 %shard_map.118 = bf16[4,16,512]{2,1,0:T(8,128)(2,1)} custom-call(s32[1]{0:T(128)S(6)} %copy.14.pick_ref, s32[1,64]{1,0:T(1,128)} %bitcast.7, bf16[64,512]{1,0:T(8,128)(2,1)} %tokens_ref.1, bf16[64,32,64]{2,1,0:T(8,128)(2,1)} %gi_hbm.1, bf16[64,32,64]{2,1,0:T(8,128)(2,1)} %ui_hbm.1, bf16[64,64,112]{2,1,0:T(8,128)(2,1)} %bitcast.4, ...), custom_call_target="tpu_custom_call" | custom-call | tf_op jit(solution)/shard_map/pallas_call | solution.py:442
  119.9 1.5 %copy.15 = bf16[64,512]{1,0:T(8,128)(2,1)} copy(bf16[64,512]{1,0:T(8,128)(2,1)} %bitcast.6) | data formatting | bytes 131072

commit v4 on v3

--- a/solution.py
+++ b/solution.py
@@ -15,21 +15,21 @@
 A_GROUPS = (1, 3, 5)
 B_GROUPS = (0, 2, 4, 6)
 NA, NB = len(A_GROUPS), len(B_GROUPS)
-AGY = (0, 2, 4, 6)
-AGZ = (1, 3, 5)
+AGY = (0, 2, 4)
+AGZ = (1, 3, 5, 6)
 CW, CCW = 0, 1
 ORDER = (
-    ("start", 2), ("ipass",), ("tout",), ("start", 4), ("start", 5), ("start", 6), ("start", 0), ("rs", 2, 2),
-    ("start", 3), ("rs", 5, 1), ("rs", 4, 2), ("rs", 6, 2), ("rs", 5, 2), ("rs", 2, 3), ("start", 1), ("rs", 0, 2),
-    ("rs", 3, 1), ("rs", 6, 3), ("rs", 4, 3), ("rs", 5, 3), ("rs", 0, 3), ("rs", 1, 1), ("rs", 2, 4), ("rs", 4, 4),
-    ("tmid",), ("gpass",), ("rs", 0, 4), ("od",), ("rs", 1, 2), ("pass", 2), ("rs", 5, 4), ("rs", 3, 2), ("pass", 4),
-    ("gend",), ("rs", 6, 4), ("pass", 0), ("rs", 1, 3), ("mdown",), ("tend",), ("hid", 2), ("hid", 4), ("rs", 3, 3),
-    ("hid", 0), ("pass", 6), ("hid", 5), ("rs", 1, 4), ("ag", 2, 2), ("ag", 4, 2), ("rs", 3, 4), ("ag", 0, 2),
-    ("hid", 6), ("hid", 1), ("ag", 5, 1), ("ag", 2, 3), ("hid", 3), ("ag", 0, 3), ("ag", 6, 2), ("ag", 1, 1),
-    ("ag", 5, 2), ("ag", 3, 1), ("ag", 6, 3), ("ag", 2, 4), ("ag", 4, 3), ("ag", 1, 2), ("down", 0), ("ag", 0, 4),
-    ("ag", 3, 2), ("ag", 2, 5), ("ag", 6, 4), ("ag", 5, 3), ("ag", 4, 4), ("ag", 1, 3), ("ag", 3, 3), ("down", 1),
-    ("ag", 5, 4), ("ag", 6, 5), ("down", 2), ("ag", 1, 4), ("ag", 0, 5), ("ag", 3, 4), ("ag", 4, 5), ("ag", 5, 5),
-    ("down", 3), ("ag", 1, 5), ("ag", 3, 5), ("down", 4),
+    ("start", 0), ("start", 2), ("start", 6), ("start", 5), ("start", 4), ("rs", 0, 2), ("start", 3), ("ipass",),
+    ("rs", 2, 2), ("rs", 4, 2), ("rs", 6, 2), ("rs", 5, 1), ("rs", 0, 3), ("rs", 2, 3), ("tout",), ("rs", 3, 1),
+    ("rs", 6, 3), ("rs", 5, 2), ("start", 1), ("rs", 0, 4), ("rs", 3, 2), ("rs", 2, 4), ("rs", 1, 1), ("rs", 5, 3),
+    ("rs", 4, 3), ("rs", 6, 4), ("gpass",), ("pass", 2), ("rs", 1, 2), ("pass", 0), ("tmid",), ("od",), ("rs", 3, 3),
+    ("rs", 5, 4), ("rs", 4, 4), ("gend",), ("pass", 6), ("tend",), ("rs", 1, 3), ("hid", 0), ("rs", 3, 4), ("hid", 2),
+    ("hid", 5), ("hid", 6), ("pass", 4), ("ag", 0, 2), ("rs", 1, 4), ("ag", 2, 2), ("hid", 3), ("ag", 5, 1),
+    ("ag", 6, 1), ("mdown",), ("hid", 4), ("ag", 0, 3), ("hid", 1), ("ag", 2, 3), ("ag", 3, 1), ("ag", 5, 2),
+    ("ag", 4, 2), ("ag", 6, 2), ("ag", 1, 1), ("ag", 2, 4), ("ag", 3, 2), ("ag", 4, 3), ("ag", 5, 3), ("down", 0),
+    ("ag", 1, 2), ("ag", 6, 3), ("ag", 0, 4), ("down", 1), ("ag", 3, 3), ("ag", 4, 4), ("ag", 1, 3), ("ag", 2, 5),
+    ("down", 2), ("ag", 5, 4), ("ag", 6, 4), ("ag", 0, 5), ("ag", 3, 4), ("ag", 4, 5), ("ag", 1, 4), ("down", 3),
+    ("ag", 3, 5), ("ag", 6, 5), ("ag", 5, 5), ("ag", 1, 5), ("down", 4),
 )
 T00 = (((0,), (0,)), ((), ()))
 T11 = (((1,), (1,)), ((), ()))

time: 122 us -> 119 us (0.975)
  Pallas kernels: 119 us -> 117 us
    pallas_call x1, Pallas kernels: 119 us -> 117 us  [layer(): pl.pallas_call(kernel, out_shape=jax.ShapeDtypeStruct((4, 16, 512), BF),...]
where the time goes in v4:
time: 119 us
  Pallas kernels  117 us (98%)
  local copies, waits for them, and re-layouts  1.47 us (1%)
    pallas_call x1, Pallas kernels, layer(): pl.pallas_call(kernel, out_shape=jax.ShapeDtypeStruct((4, 16, 512), BF),...  117 us

profile of v4, /device:TPU:1, one launch (start us, length us, event | category | flops | bytes accessed | tf_op | source)
XLA Modules:
  0.0 118.7 jit_solution(10378283127971524482)
XLA Ops:
  0.7 116.6 %shard_map.118 = bf16[4,16,512]{2,1,0:T(8,128)(2,1)} custom-call(s32[1]{0:T(128)S(6)} %copy.14.pick_ref, s32[1,64]{1,0:T(1,128)} %bitcast.7, bf16[64,512]{1,0:T(8,128)(2,1)} %tokens_ref.1, bf16[64,32,64]{2,1,0:T(8,128)(2,1)} %gi_hbm.1, bf16[64,32,64]{2,1,0:T(8,128)(2,1)} %ui_hbm.1, bf16[64,64,112]{2,1,0:T(8,128)(2,1)} %bitcast.4, ...), custom_call_target="tpu_custom_call" | custom-call | tf_op jit(solution)/shard_map/pallas_call | solution.py:442
  117.3 1.5 %copy.15 = bf16[64,512]{1,0:T(8,128)(2,1)} copy(bf16[64,512]{1,0:T(8,128)(2,1)} %bitcast.6) | data formatting | bytes 131072

commit v5 on v4

--- a/solution.py
+++ b/solution.py
@@ -19,17 +19,17 @@
 AGZ = (1, 3, 5, 6)
 CW, CCW = 0, 1
 ORDER = (
-    ("start", 0), ("start", 2), ("start", 6), ("start", 5), ("start", 4), ("rs", 0, 2), ("start", 3), ("ipass",),
-    ("rs", 2, 2), ("rs", 4, 2), ("rs", 6, 2), ("rs", 5, 1), ("rs", 0, 3), ("rs", 2, 3), ("tout",), ("rs", 3, 1),
-    ("rs", 6, 3), ("rs", 5, 2), ("start", 1), ("rs", 0, 4), ("rs", 3, 2), ("rs", 2, 4), ("rs", 1, 1), ("rs", 5, 3),
-    ("rs", 4, 3), ("rs", 6, 4), ("gpass",), ("pass", 2), ("rs", 1, 2), ("pass", 0), ("tmid",), ("od",), ("rs", 3, 3),
-    ("rs", 5, 4), ("rs", 4, 4), ("gend",), ("pass", 6), ("tend",), ("rs", 1, 3), ("hid", 0), ("rs", 3, 4), ("hid", 2),
-    ("hid", 5), ("hid", 6), ("pass", 4), ("ag", 0, 2), ("rs", 1, 4), ("ag", 2, 2), ("hid", 3), ("ag", 5, 1),
-    ("ag", 6, 1), ("mdown",), ("hid", 4), ("ag", 0, 3), ("hid", 1), ("ag", 2, 3), ("ag", 3, 1), ("ag", 5, 2),
-    ("ag", 4, 2), ("ag", 6, 2), ("ag", 1, 1), ("ag", 2, 4), ("ag", 3, 2), ("ag", 4, 3), ("ag", 5, 3), ("down", 0),
-    ("ag", 1, 2), ("ag", 6, 3), ("ag", 0, 4), ("down", 1), ("ag", 3, 3), ("ag", 4, 4), ("ag", 1, 3), ("ag", 2, 5),
-    ("down", 2), ("ag", 5, 4), ("ag", 6, 4), ("ag", 0, 5), ("ag", 3, 4), ("ag", 4, 5), ("ag", 1, 4), ("down", 3),
-    ("ag", 3, 5), ("ag", 6, 5), ("ag", 5, 5), ("ag", 1, 5), ("down", 4),
+    ("start", 0), ("ipass",), ("gpass",), ("start", 4), ("start", 6), ("start", 2), ("start", 3), ("rs", 0, 2),
+    ("rs", 4, 2), ("rs", 2, 2), ("rs", 3, 1), ("rs", 6, 2), ("start", 1), ("od",), ("rs", 0, 3), ("rs", 4, 3),
+    ("tout",), ("rs", 2, 3), ("rs", 0, 4), ("rs", 6, 3), ("rs", 1, 1), ("rs", 3, 2), ("start", 5), ("rs", 4, 4),
+    ("rs", 2, 4), ("rs", 5, 1), ("rs", 3, 3), ("rs", 1, 2), ("tmid",), ("mdown",), ("rs", 6, 4), ("pass", 0),
+    ("pass", 4), ("gend",), ("rs", 5, 2), ("pass", 2), ("tend",), ("rs", 3, 4), ("rs", 1, 3), ("hid", 0), ("pass", 6),
+    ("hid", 4), ("rs", 5, 3), ("hid", 2), ("rs", 1, 4), ("hid", 3), ("ag", 0, 2), ("ag", 4, 2), ("hid", 6),
+    ("ag", 2, 2), ("rs", 5, 4), ("hid", 1), ("ag", 3, 1), ("ag", 4, 3), ("ag", 0, 3), ("ag", 6, 1), ("ag", 2, 3),
+    ("hid", 5), ("ag", 1, 1), ("ag", 3, 2), ("ag", 4, 4), ("ag", 0, 4), ("ag", 6, 2), ("ag", 5, 1), ("ag", 1, 2),
+    ("ag", 2, 4), ("down", 0), ("ag", 3, 3), ("ag", 4, 5), ("ag", 5, 2), ("ag", 1, 3), ("ag", 6, 3), ("down", 1),
+    ("ag", 2, 5), ("ag", 5, 3), ("ag", 0, 5), ("ag", 3, 4), ("ag", 1, 4), ("down", 2), ("ag", 6, 4), ("ag", 5, 4),
+    ("down", 3), ("ag", 1, 5), ("ag", 3, 5), ("ag", 6, 5), ("ag", 5, 5), ("down", 4),
 )
 T00 = (((0,), (0,)), ((), ()))
 T11 = (((1,), (1,)), ((), ()))

time: 119 us -> 118 us (level)
  no operation moved by 1% of the time
where the time goes in v5:
time: 118 us
  Pallas kernels  116 us (98%)
  local copies, waits for them, and re-layouts  1.47 us (1%)
    pallas_call x1, Pallas kernels, layer(): pl.pallas_call(kernel, out_shape=jax.ShapeDtypeStruct((4, 16, 512), BF),...  116 us

profile of v5, /device:TPU:1, one launch (start us, length us, event | category | flops | bytes accessed | tf_op | source)
XLA Modules:
  0.0 118.0 jit_solution(13830096581752106951)
XLA Ops:
  0.7 115.8 %shard_map.118 = bf16[4,16,512]{2,1,0:T(8,128)(2,1)} custom-call(s32[1]{0:T(128)S(6)} %copy.14.pick_ref, s32[1,64]{1,0:T(1,128)} %bitcast.7, bf16[64,512]{1,0:T(8,128)(2,1)} %tokens_ref.1, bf16[64,32,64]{2,1,0:T(8,128)(2,1)} %gi_hbm.1, bf16[64,32,64]{2,1,0:T(8,128)(2,1)} %ui_hbm.1, bf16[64,64,112]{2,1,0:T(8,128)(2,1)} %bitcast.4, ...), custom_call_target="tpu_custom_call" | custom-call | tf_op jit(solution)/shard_map/pallas_call | solution.py:442
  116.5 1.5 %copy.15 = bf16[64,512]{1,0:T(8,128)(2,1)} copy(bf16[64,512]{1,0:T(8,128)(2,1)} %bitcast.6) | data formatting | bytes 131072
